TPU v7x, 32 devices: a whole 2x2x4 slice. The times are simulated.
32 devices in a mesh: wall: 4 (over x, core), span: 4 (over z), stream: 2 (over y).
Axes of the slice: x: 2, y: 2, z: 4, core: 2. Of those that a mesh axis runs over, the one named last changes fastest.
Arguments:
- right_side: float32 [4, 2, 8, 64, 320], P('span', 'stream', 'wall'), may hold values from -6 to 6
- old_values: float32 [4, 2, 8, 64, 320], P('span', 'stream', 'wall'), may hold values from -6 to 6
- element_library: float32 [8, 320], replicated, as said below
- wall_library: float32 [3, 320, 320], replicated, as said below
- face_library: float32 [4, 320, 320], replicated, may hold values from -0.15625 to 0.15625
- element_index: int32 [4, 2, 8], P('span', 'stream', 'wall'), may hold values from 0 to 7
- wall_faces: int32 [4, 2, 8, 2], P('span', 'stream', 'wall'), may hold values from 0 to 2, as said below
- face_index: int32 [4, 2, 8, 4], P('span', 'stream', 'wall'), may hold values from 0 to 3
Outputs:
- new_values: float32 [4, 2, 8, 64, 320], P('span', 'stream', 'wall')
Inputs may be any that keep to these rules, and one draw needn't show every extreme that they name: On every line wall_faces[..., i, 1] equals wall_faces[..., i + 1, 0] for i < 7. `wall_library`: every block is symmetric positive definite. `element_library`: entries are positive.
All inputs are finite; a program needn't handle non-finite values.
Results may differ from a plain program's by a relative error of at most 0.0003.
Values sent between devices are 32-bit elements; how exact they have to be, the bound alone decides.
A program may use at most 64 MiB of HBM per device.

v0:
```python
import jax
import jax.numpy as jnp
from jax import lax
from jax.sharding import PartitionSpec as P

HIGHEST = lax.Precision.HIGHEST


def padded_2(cells, sides, width):
    for axis, dim in sides:
        count = lax.axis_size(axis)
        head = lax.slice_in_dim(cells, 0, width, axis=dim)
        tail = lax.slice_in_dim(cells, cells.shape[dim] - width, cells.shape[dim], axis=dim)
        cells = jnp.concatenate(
            [
                lax.ppermute(tail, axis, [(i, (i + 1) % count) for i in range(count)]),
                cells,
                lax.ppermute(head, axis, [((i + 1) % count, i) for i in range(count)]),
            ],
            axis=dim,
        )
    return cells


def lower_solve(factor, values):
    return jax.scipy.linalg.solve_triangular(factor, values, lower=True)


def upper_solve(factor, values):
    return jax.scipy.linalg.solve_triangular(factor, values, lower=True, trans=1)


def coupled_sum(index_rows, near_rows, face_library):

    def one_element(per_element):
        index_row, near_now = per_element
        return jnp.einsum("djk,dvk->jv", face_library[index_row], near_now, precision=HIGHEST)

    return lax.map(one_element, (index_rows, near_rows))


def eliminate(
    element_rates, prev_faces, next_faces, residual_t, wall_library, factor_in, carried_in
):
    element_count = element_rates.shape[0]
    link_flags = jnp.ones((element_count,), jnp.float32)
    link_flags = link_flags.at[0].set(0.0)

    def advance_one(carried_state, per_element):
        factor_prev, carried_prev, unused_pivot = carried_state
        rate_row, prev_face, next_face, residual_row, link_flag = per_element
        coupling = wall_library[prev_face]
        scaled = lower_solve(factor_prev, coupling)
        reduced = lower_solve(factor_prev, carried_prev)
        pivot_now = (
            jnp.diag(rate_row)
            + coupling
            + wall_library[next_face]
            - link_flag * jnp.dot(scaled.T, scaled, precision=HIGHEST)
        )
        carried = residual_row + link_flag * jnp.dot(scaled.T, reduced, precision=HIGHEST)
        factor = jnp.linalg.cholesky(pivot_now)
        return ((factor, carried, pivot_now), (factor, carried))

    start_carry = (factor_in, carried_in, jnp.zeros_like(factor_in))
    last_state, (factors, carries) = lax.scan(
        advance_one, start_carry, (element_rates, prev_faces, next_faces, residual_t, link_flags)
    )
    return (factors, carries, last_state[0], last_state[1], last_state[2])


def substitute(factors, carries, prev_faces, wall_library, term_in):

    def retreat_one(term_next, per_element):
        factor, carried, prev_face = per_element
        solution = upper_solve(factor, lower_solve(factor, carried + term_next))
        return (jnp.dot(wall_library[prev_face], solution, precision=HIGHEST), solution)

    term_first, solutions = lax.scan(
        retreat_one, term_in, (factors, carries, prev_faces), reverse=True
    )
    return (solutions, term_first)


def substructure(
    element_rates, below_faces, above_faces, residual_t, wall_library, wall_position, wall_count
):
    element_count = residual_t.shape[0]
    unknowns = residual_t.shape[1]
    vector_count = residual_t.shape[2]
    inner = element_count - 1
    identity = jnp.eye(unknowns, dtype=jnp.float32)
    spike = jnp.zeros((inner, unknowns, unknowns), jnp.float32).at[0].set(identity)
    widened = jnp.concatenate([residual_t[:inner], spike], axis=2)
    zero_wide = jnp.zeros((unknowns, vector_count + unknowns), jnp.float32)
    factors, carries, unused_factor, unused_carried, unused_pivot = eliminate(
        element_rates[:inner],
        below_faces[:inner],
        above_faces[:inner],
        widened,
        wall_library,
        identity,
        zero_wide,
    )
    solved, unused_term = substitute(factors, carries, below_faces[:inner], wall_library, zero_wide)
    local_solution = solved[:, :, :vector_count]
    first_column = solved[:, :, vector_count:]
    lower_face = wall_library[below_faces[0]]
    upper_face = wall_library[below_faces[inner]]
    scaled_upper = lower_solve(factors[inner - 1], upper_face)
    own_block = (
        jnp.diag(element_rates[inner])
        + upper_face
        + wall_library[above_faces[inner]]
        - jnp.dot(scaled_upper.T, scaled_upper, precision=HIGHEST)
    )
    from_first = jnp.dot(
        lower_face, jnp.dot(first_column[0], lower_face, precision=HIGHEST), precision=HIGHEST
    )
    across = -jnp.dot(
        lower_face,
        jnp.dot(first_column[inner - 1].T, upper_face, precision=HIGHEST),
        precision=HIGHEST,
    )
    own_side = residual_t[inner] + jnp.dot(upper_face, local_solution[inner - 1], precision=HIGHEST)
    side_below = jnp.dot(lower_face, local_solution[0], precision=HIGHEST)
    own_all, first_all, across_all, side_all, below_all = (
        lax.all_gather(own_block[None], "wall", axis=0, tiled=True),
        lax.all_gather(from_first[None], "wall", axis=0, tiled=True),
        lax.all_gather(across[None], "wall", axis=0, tiled=True),
        lax.all_gather(own_side[None], "wall", axis=0, tiled=True),
        lax.all_gather(side_below[None], "wall", axis=0, tiled=True),
    )
    pivot_factors = []
    carried_list = []
    for place in range(wall_count):
        diagonal_block = own_all[place]
        side_now = side_all[place]
        if place + 1 < wall_count:
            diagonal_block = diagonal_block - first_all[place + 1]
            side_now = side_now + below_all[place + 1]
        if place > 0:
            scaled = lower_solve(pivot_factors[place - 1], across_all[place])
            reduced = lower_solve(pivot_factors[place - 1], carried_list[place - 1])
            diagonal_block = diagonal_block - jnp.dot(scaled.T, scaled, precision=HIGHEST)
            side_now = side_now - jnp.dot(scaled.T, reduced, precision=HIGHEST)
        pivot_factors.append(jnp.linalg.cholesky(diagonal_block))
        carried_list.append(side_now)
    separators = [None] * wall_count
    for place in range(wall_count - 1, -1, -1):
        side_now = carried_list[place]
        if place + 1 < wall_count:
            side_now = side_now - jnp.dot(
                across_all[place + 1], separators[place + 1], precision=HIGHEST
            )
        separators[place] = upper_solve(
            pivot_factors[place], lower_solve(pivot_factors[place], side_now)
        )
    stacked = jnp.stack(separators, axis=0)
    sep_above = lax.dynamic_index_in_dim(stacked, wall_position, 0, keepdims=False)
    below_place = jnp.maximum(wall_position - 1, 0)
    sep_below = lax.dynamic_index_in_dim(stacked, below_place, 0, keepdims=False) * (
        wall_position > 0
    ).astype(jnp.float32)
    interior, unused_first = substitute(
        factors,
        carries[:, :, :vector_count],
        below_faces[:inner],
        wall_library,
        jnp.dot(upper_face, sep_above, precision=HIGHEST),
    )
    pushed = jnp.dot(lower_face, sep_below, precision=HIGHEST)
    interior = interior + jnp.einsum("ejk,kv->ejv", first_column, pushed, precision=HIGHEST)
    return jnp.concatenate([interior, sep_above[None]], axis=0)


def on_device(
    right_side,
    old_values,
    element_library,
    wall_library,
    face_library,
    element_index,
    wall_faces,
    face_index,
):
    local_side = right_side[0, 0]
    padded = padded_2(old_values, (("span", 0), ("stream", 1)), 1)
    near_rows = jnp.stack([padded[0, 1], padded[2, 1], padded[1, 0], padded[1, 2]], axis=1)
    coupled = coupled_sum(face_index[0, 0], near_rows, face_library)
    residual_t = jnp.swapaxes(local_side, 1, 2) - coupled
    library_row_list = jnp.arange(element_library.shape[0], dtype=jnp.int32)
    selector = (element_index[0, 0][:, None] == library_row_list[None, :]).astype(jnp.float32)
    element_rates = jnp.dot(selector, element_library, precision=HIGHEST)
    below_faces = wall_faces[0, 0, :, 0]
    above_faces = wall_faces[0, 0, :, 1]
    wall_position = lax.axis_index("wall")
    wall_count = lax.axis_size("wall")
    physical = substructure(
        element_rates, below_faces, above_faces, residual_t, wall_library, wall_position, wall_count
    )
    return jnp.swapaxes(physical, 1, 2)[None, None]


def solution(mesh):
    placed = (
        P("span", "stream", "wall", None, None),
        P("span", "stream", "wall", None, None),
        P(),
        P(),
        P(),
        P("span", "stream", "wall"),
        P("span", "stream", "wall", None),
        P("span", "stream", "wall", None),
    )
    return jax.shard_map(
        on_device,
        mesh=mesh,
        in_specs=placed,
        out_specs=P("span", "stream", "wall", None, None),
        check_vma=False,
    )
```

profile of v0, /device:TPU:0, one launch (start us, length us, event | category | flops | bytes accessed | tf_op | source)
XLA Modules:
  0.0 770.9 jit_solution(17472146189807102540)
XLA Ops:
  22.8 30.4 %custom-call.56 = f32[3,128,128]{1,2,0:T(8,128)} custom-call(f32[3,128,128]{2,1,0:T(8,128)S(1)} %pad_maximum_fusion.14), custom_call_target="InvertDiagBlocksLowerTriangular" | custom-call | tf_op jit(solution)/shard_map/while/body/eval_jaxpr/jit(_solve_triangular)/triangular_solve | solution.py:26
  62.6 11.7 %cholesky.421 = f32[128,128]{1,0:T(8,128)S(1)} custom-call(f32[128,128]{1,0:T(8,128)S(1)} %copy.63), custom_call_target="Cholesky" | custom-call | tf_op jit(solution)/shard_map/while/body/eval_jaxpr/jit(cholesky)/cholesky | solution.py:62
  86.8 12.2 %cholesky.440 = f32[128,128]{1,0:T(8,128)S(1)} custom-call(f32[128,128]{1,0:T(8,128)S(1)} %copy.65), custom_call_target="Cholesky" | custom-call | tf_op jit(solution)/shard_map/while/body/eval_jaxpr/jit(cholesky)/cholesky | solution.py:62
  99.1 9.8 %custom-call.58 = f32[1,128,128]{1,2,0:T(8,128)S(1)} custom-call(f32[1,128,128]{2,1,0:T(8,128)S(1)} %get-tuple-element.423), custom_call_target="InvertDiagBlocksLowerTriangular" | custom-call | tf_op jit(solution)/shard_map/while/body/eval_jaxpr/jit(cholesky)/cholesky | solution.py:62
  125.3 30.3 %custom-call.85 = f32[3,128,128]{1,2,0:T(8,128)S(1)} custom-call(f32[3,128,128]{2,1,0:T(8,128)} %pad_maximum_fusion.15), custom_call_target="InvertDiagBlocksLowerTriangular" | custom-call | tf_op jit(solution)/shard_map/while/body/eval_jaxpr/jit(_solve_triangular)/triangular_solve | solution.py:30
  187.3 11.1 %collective-permute-done.2 = f32[3,1,2,64,320]{4,3,2,1,0:T(8,128)S(1)} collective-permute-done((f32[3,1,2,64,320]{4,3,2,1,0:T(8,128)}, f32[3,1,2,64,320]{4,3,2,1,0:T(8,128)S(1)}, u32[]{:S(2)}, u32[]{:S(2)}) %collective-permute-start.2) | collective-permute-done | bytes 491552 | tf_op jit(solution)/shard_map/ppermute | solution.py:16
  200.4 11.3 %while.70 = (s32[]{:T(128)}, f32[2,320,64]{1,2,0:T(8,128)}, s32[2,4]{1,0:T(2,128)S(1)}, f32[4,320,320]{2,1,0:T(8,128)}, f32[2,4,64,320]{3,2,1,0:T(8,128)}, /*index=5*/s32[]{:T(128)}) while((s32[]{:T(128)}, f32[2,320,64]{1,2,0:T(8,128)}, s32[2,4]{1,0:T(2,128)S(1)}, f32[4,320,320]{2,1,0:T(8,128)}, f32[2,4,64,320]{3,2,1,0:T(8,128)}, ...), condition=%wide.region_7.10_spmd, body=%wide.region_6.9_spmd.sunk | while | flops 314573824 | bytes 5411977 | solution.py:39
  256.6 11.7 %cholesky.478 = f32[128,128]{1,0:T(8,128)S(1)} custom-call(f32[128,128]{1,0:T(8,128)S(1)} %cholesky.710), custom_call_target="Cholesky" | custom-call | tf_op jit(solution)/shard_map/jit(cholesky)/cholesky | solution.py:147
  280.6 12.1 %cholesky.497 = f32[128,128]{1,0:T(8,128)S(1)} custom-call(f32[128,128]{1,0:T(8,128)S(1)} %cholesky.714), custom_call_target="Cholesky" | custom-call | tf_op jit(solution)/shard_map/jit(cholesky)/cholesky | solution.py:147
  317.7 29.7 %custom-call.83 = f32[3,128,128]{1,2,0:T(8,128)S(1)} custom-call(f32[3,128,128]{2,1,0:T(8,128)S(1)} %pad_maximum_fusion.16), custom_call_target="InvertDiagBlocksLowerTriangular" | custom-call | tf_op jit(solution)/shard_map/jit(_solve_triangular)/triangular_solve | solution.py:30
  359.1 11.7 %cholesky.535 = f32[128,128]{1,0:T(8,128)S(1)} custom-call(f32[128,128]{1,0:T(8,128)S(1)} %cholesky.718), custom_call_target="Cholesky" | custom-call | tf_op jit(solution)/shard_map/jit(cholesky)/cholesky | solution.py:147
  383.2 13.4 %cholesky.554 = f32[128,128]{1,0:T(8,128)} custom-call(f32[128,128]{1,0:T(8,128)} %cholesky.722), custom_call_target="Cholesky" | custom-call | tf_op jit(solution)/shard_map/jit(cholesky)/cholesky | solution.py:147
  399.4 11.3 %custom-call.66 = f32[1,128,128]{1,2,0:T(8,128)} custom-call(f32[1,128,128]{2,1,0:T(8,128)} %get-tuple-element.413), custom_call_target="InvertDiagBlocksLowerTriangular" | custom-call | tf_op jit(solution)/shard_map/jit(cholesky)/cholesky | solution.py:147
  434.4 31.3 %custom-call.81 = f32[3,128,128]{1,2,0:T(8,128)} custom-call(f32[3,128,128]{2,1,0:T(8,128)} %pad_maximum_fusion.17), custom_call_target="InvertDiagBlocksLowerTriangular" | custom-call | tf_op jit(solution)/shard_map/jit(_solve_triangular)/triangular_solve | solution.py:30
  491.2 13.2 %cholesky.592 = f32[128,128]{1,0:T(8,128)} custom-call(f32[128,128]{1,0:T(8,128)} %cholesky.726), custom_call_target="Cholesky" | custom-call | tf_op jit(solution)/shard_map/jit(cholesky)/cholesky | solution.py:147
  507.5 11.3 %custom-call.69 = f32[1,128,128]{1,2,0:T(8,128)} custom-call(f32[1,128,128]{2,1,0:T(8,128)} %get-tuple-element.411), custom_call_target="InvertDiagBlocksLowerTriangular" | custom-call | tf_op jit(solution)/shard_map/jit(cholesky)/cholesky | solution.py:147
  523.0 13.3 %cholesky.611 = f32[128,128]{1,0:T(8,128)} custom-call(f32[128,128]{1,0:T(8,128)} %cholesky.730), custom_call_target="Cholesky" | custom-call | tf_op jit(solution)/shard_map/jit(cholesky)/cholesky | solution.py:147
  539.1 11.3 %custom-call.70 = f32[1,128,128]{1,2,0:T(8,128)} custom-call(f32[1,128,128]{2,1,0:T(8,128)} %get-tuple-element.408), custom_call_target="InvertDiagBlocksLowerTriangular" | custom-call | tf_op jit(solution)/shard_map/jit(cholesky)/cholesky | solution.py:147
  573.9 31.1 %custom-call.79 = f32[3,128,128]{1,2,0:T(8,128)} custom-call(f32[3,128,128]{2,1,0:T(8,128)} %pad_maximum_fusion.18), custom_call_target="InvertDiagBlocksLowerTriangular" | custom-call | tf_op jit(solution)/shard_map/jit(_solve_triangular)/triangular_solve | solution.py:30
  625.2 13.2 %cholesky.649 = f32[128,128]{1,0:T(8,128)} custom-call(f32[128,128]{1,0:T(8,128)} %cholesky.734), custom_call_target="Cholesky" | custom-call | tf_op jit(solution)/shard_map/jit(cholesky)/cholesky | solution.py:147
  641.5 11.3 %custom-call.73 = f32[1,128,128]{1,2,0:T(8,128)} custom-call(f32[1,128,128]{2,1,0:T(8,128)} %get-tuple-element.406), custom_call_target="InvertDiagBlocksLowerTriangular" | custom-call | tf_op jit(solution)/shard_map/jit(cholesky)/cholesky | solution.py:147
  657.0 13.6 %cholesky.668 = f32[128,128]{1,0:T(8,128)} custom-call(f32[128,128]{1,0:T(8,128)} %cholesky.738), custom_call_target="Cholesky" | custom-call | tf_op jit(solution)/shard_map/jit(cholesky)/cholesky | solution.py:147
  673.4 11.3 %custom-call.74 = f32[1,128,128]{1,2,0:T(8,128)} custom-call(f32[1,128,128]{2,1,0:T(8,128)} %get-tuple-element.403), custom_call_target="InvertDiagBlocksLowerTriangular" | custom-call | tf_op jit(solution)/shard_map/jit(cholesky)/cholesky | solution.py:147
  708.3 31.1 %custom-call.77 = f32[3,128,128]{1,2,0:T(8,128)} custom-call(f32[3,128,128]{2,1,0:T(8,128)} %pad_maximum_fusion.19), custom_call_target="InvertDiagBlocksLowerTriangular" | custom-call | tf_op jit(solution)/shard_map/jit(_solve_triangular)/triangular_solve | solution.py:30
  (460 shorter events, 384.0 us)
Async XLA Ops:
  6.5 51.0 %copy-start = (f32[8,320]{1,0:T(8,128)S(1)}, f32[8,320]{1,0:T(8,128)}, u32[]{:S(2)}) copy-start(f32[8,320]{1,0:T(8,128)} %param.25) | copy-start | bytes 30724
  6.5 47.9 %copy-start.19 = (f32[3,320,320]{2,1,0:T(8,128)S(1)}, f32[3,320,320]{2,1,0:T(8,128)}, u32[]{:S(2)}) copy-start(f32[3,320,320]{2,1,0:T(8,128)} %param.26) | copy-start | bytes 3686404
  6.5 238.0 %all-gather.11.cloned.1.call-start = ((), (), s32[]{:S(2)}) async-start(), calls=%async_computation | async-start | bytes 2457600 | tf_op jit(solution)/shard_map/all_gather | solution.py:128
  6.5 160.2 %collective-permute-start = (f32[1,1,2,64,320]{4,3,2,1,0:T(8,128)}, f32[1,1,2,64,320]{4,3,2,1,0:T(8,128)}, u32[]{:S(2)}, u32[]{:S(2)}) collective-permute-start(f32[1,1,2,64,320]{4,3,2,1,0:T(8,128)} %param.24), channel_id=1, source_target_pairs={{0,2},{2,4},{4,6},{6,0},{1,3},{3,5},{5,7},{7,1},{8,10},{10,12},{12... | collective-permute-start | bytes 491528 | tf_op jit(solution)/shard_map/ppermute | solution.py:16
  9.6 159.6 %collective-permute-start.1 = (f32[1,1,2,64,320]{4,3,2,1,0:T(8,128)}, f32[1,1,2,64,320]{4,3,2,1,0:T(8,128)}, u32[]{:S(2)}, u32[]{:S(2)}) collective-permute-start(f32[1,1,2,64,320]{4,3,2,1,0:T(8,128)} %param.24), channel_id=1, source_target_pairs={{2,0},{4,2},{6,4},{0,6},{3,1},{5,3},{7,5},{1,7},{10,8},{12,10},{14... | collective-permute-start | bytes 491528 | tf_op jit(solution)/shard_map/ppermute | solution.py:18
  22.7 34.0 %copy-start.22 = (f32[320,320]{1,0:T(8,128)}, f32[320,320]{1,0:T(8,128)S(1)}, u32[]{:S(2)}) copy-start(f32[320,320]{1,0:T(8,128)S(1)} %get-tuple-element.775) | copy-start | bytes 1228804
  124.4 94.5 %copy-start.1 = (f32[320,320]{1,0:T(8,128)}, f32[320,320]{1,0:T(8,128)S(1)}, u32[]{:S(2)}) copy-start(f32[320,320]{1,0:T(8,128)S(1)} %get-tuple-element.769) | copy-start | bytes 1228804
  162.9 12.0 %copy-start.52 = (f32[1,1,2,64,320]{4,3,2,1,0:T(8,128)S(1)}, f32[1,1,2,64,320]{4,3,2,1,0:T(8,128)}, u32[]{:S(2)}) copy-start(f32[1,1,2,64,320]{4,3,2,1,0:T(8,128)} %param.23) | copy-start | bytes 491524
  162.9 88.3 %all-gather.13.cloned.1.call-start = ((), (), s32[]{:S(2)}) async-start(), calls=%async_computation.1 | async-start | bytes 2457600 | tf_op jit(solution)/shard_map/all_gather | solution.py:129
  164.3 8.2 %copy-start.15 = (f32[128,384]{1,0:T(8,128)}, f32[128,384]{1,0:T(8,128)S(1)}, u32[]{:S(2)}) copy-start(f32[128,384]{1,0:T(8,128)S(1)} %fusion.103) | copy-start | bytes 589828
  170.8 29.6 %copy-start.53 = (s32[1,1,2,4]{3,2,1,0:T(2,128)S(1)}, s32[1,1,2,4]{3,2,1,0:T(2,128)}, u32[]{:S(2)}) copy-start(s32[1,1,2,4]{3,2,1,0:T(2,128)} %param.30) | copy-start | bytes 100
  170.8 16.5 %collective-permute-start.3 = (f32[3,1,2,64,320]{4,3,2,1,0:T(8,128)}, f32[3,1,2,64,320]{4,3,2,1,0:T(8,128)S(1)}, u32[]{:S(2)}, u32[]{:S(2)}) collective-permute-start(f32[3,1,2,64,320]{4,3,2,1,0:T(8,128)} %constant_dynamic-update-slice_fusion), channel_id=1, source_target_pairs={{1,0},{0,1},{3,2},{2,3},{5,4},{4,5},{7,6},{6,7},{9,8},{8,9},{11,10... | collective-permute-start | bytes 1474568 | tf_op jit(solution)/shard_map/ppermute | solution.py:18
  173.7 24.8 %collective-permute-start.2 = (f32[3,1,2,64,320]{4,3,2,1,0:T(8,128)}, f32[3,1,2,64,320]{4,3,2,1,0:T(8,128)S(1)}, u32[]{:S(2)}, u32[]{:S(2)}) collective-permute-start(f32[3,1,2,64,320]{4,3,2,1,0:T(8,128)} %constant_dynamic-update-slice_fusion), channel_id=1, source_target_pairs={{0,1},{1,0},{2,3},{3,2},{4,5},{5,4},{6,7},{7,6},{8,9},{9,8},{10,11... | collective-permute-start | bytes 1474568 | tf_op jit(solution)/shard_map/ppermute | solution.py:16
  222.8 125.6 %all-gather.15.cloned.1.call-start = ((), (), s32[]{:S(2)}) async-start(), calls=%async_computation.2 | async-start | bytes 2457600 | tf_op jit(solution)/shard_map/all_gather | solution.py:130
  229.9 9.9 %copy-start.40 = (f32[4,320,64]{1,2,0:T(8,128)}, f32[4,320,64]{1,2,0:T(8,128)S(1)}, u32[]{:S(2)}) copy-start(f32[4,320,64]{1,2,0:T(8,128)S(1)} %all-gather.5) | copy-start | bytes 983044
  278.2 69.1 %copy-start.44 = (f32[320,64]{0,1:T(8,128)S(1)}, f32[320,64]{0,1:T(8,128)}, u32[]{:S(2)}) copy-start(f32[320,64]{0,1:T(8,128)} %fusion.82) | copy-start | bytes 245764
  317.6 36.7 %copy-start.6 = (f32[320,320]{1,0:T(8,128)}, f32[320,320]{1,0:T(8,128)S(1)}, u32[]{:S(2)}) copy-start(f32[320,320]{1,0:T(8,128)S(1)} %get-tuple-element.771) | copy-start | bytes 1228804
  359.0 21.9 %copy-start.36 = (f32[320,320]{1,0:T(8,128)}, f32[320,320]{1,0:T(8,128)S(1)}, u32[]{:S(2)}) copy-start(f32[320,320]{1,0:T(8,128)S(1)} %fusion.25) | copy-start | bytes 1228804
  382.6 88.9 %copy-start.3 = (f32[1280,320]{1,0:T(8,128)S(1)}, f32[1280,320]{1,0:T(8,128)}, u32[]{:S(2)}) copy-start(f32[1280,320]{1,0:T(8,128)} %all-gather.15.cloned.1.call-done) | copy-start | bytes 4915204
  605.0 13.6 %copy-start.29 = (f32[320,320]{0,1:T(8,128)S(1)}, f32[320,320]{0,1:T(8,128)}, u32[]{:S(2)}) copy-start(f32[320,320]{0,1:T(8,128)} %copy.110) | copy-start | bytes 1228804
  706.6 43.3 %copy-start.43 = (f32[320,64]{0,1:T(8,128)S(1)}, f32[320,64]{0,1:T(8,128)}, u32[]{:S(2)}) copy-start(f32[320,64]{0,1:T(8,128)} %convolution_subtract_fusion.29) | copy-start | bytes 245764
  739.4 11.2 %copy-start.28 = (f32[3,128,128]{1,2,0:T(8,128)S(1)}, f32[3,128,128]{1,2,0:T(8,128)}, u32[]{:S(2)}) copy-start(f32[3,128,128]{1,2,0:T(8,128)} %custom-call.79) | copy-start | bytes 589828
  739.4 11.4 %copy-start.11 = (f32[320,320]{1,0:T(8,128)S(1)}, f32[320,320]{1,0:T(8,128)}, u32[]{:S(2)}) copy-start(f32[320,320]{1,0:T(8,128)} %get-tuple-element.773) | copy-start | bytes 1228804
  740.5 12.2 %copy-start.42 = (f32[320,64]{0,1:T(8,128)S(1)}, f32[320,64]{0,1:T(8,128)}, u32[]{:S(2)}) copy-start(f32[320,64]{0,1:T(8,128)} %convolution_subtract_fusion.30) | copy-start | bytes 245764
  (38 other events, 109.4 us)
Sparse Core Ops, SparseCore 0:
  163.0 21.4 all-gather.10
  222.9 23.2 all-gather.12
  247.8 21.9 all-gather.14
where the time goes:
time: 779 us; the launch traced here: 771 us
  other arithmetic  486 us (62%)
  matrix products  127 us (16%)
  local copies, waits for them, and re-layouts  81 us (10%)
  between operations  32.4 us (4%)
  waiting for transfers between devices  21 us (3%)
  blocking collectives  15.7 us (2%)
    another operation x44, other arithmetic, substructure(): pivot_factors.append(jnp.linalg.cholesky(diagonal_block))  231 us
    another operation x20, other arithmetic, upper_solve(): jax.scipy.linalg.solve_triangular(factor, values, lower=True, trans=1)  164 us
    another operation x75, matrix products, lower_solve(): return jax.scipy.linalg.solve_triangular(factor, values, lower=True)  52.4 us
    another operation x10, other arithmetic, advance_one(): factor = jnp.linalg.cholesky(pivot_now)  50.9 us
    another operation x7, other arithmetic, lower_solve(): return jax.scipy.linalg.solve_triangular(factor, values, lower=True)  30.5 us
    another operation x35, local copies, waits for them, and re-layouts, upper_solve(): jax.scipy.linalg.solve_triangular(factor, values, lower=True, trans=1)  28.4 us
    unnamed x121, local copies, waits for them, and re-layouts  20.2 us
    another operation x16, matrix products, substructure(): pivot_factors.append(jnp.linalg.cholesky(diagonal_block))  20 us
  transfers between devices with their start and end apart: 7, of which 2 were waited for; matrix products, arithmetic and copies ran while one was open for 36% of the time, Pallas kernels for 0%

commit v1 on v0

v1 whole, which is shorter than its diff:
```python
import functools
import jax
import jax.numpy as jnp
from jax import lax
from jax.experimental import pallas as pl
from jax.experimental.pallas import tpu as pltpu
from jax.sharding import PartitionSpec as P

F32 = jnp.float32
BF16 = jnp.bfloat16
LOW_STEPS = 4
HIGH_STEPS = 4
CONVERGED = 3e-3


def dot(a, b, transposed=False):
    dims = (((1,), (1,)), ((), ())) if transposed else (((1,), (0,)), ((), ()))
    return lax.dot_general(a, b, dims, preferred_element_type=F32)


def split(a):
    high = a.astype(BF16)
    return high, (a - high.astype(F32)).astype(BF16)


def dot3(a, b, transposed=False):
    return (
        dot(a[0], b[0], transposed) + (dot(a[0], b[1], transposed) + dot(a[1], b[0], transposed))
    )


def eye_mask(size):
    row = lax.broadcasted_iota(jnp.int32, (size, size), 0)
    col = lax.broadcasted_iota(jnp.int32, (size, size), 1)
    return row == col


def gauss_jordan(a_ref, x_ref):
    size = a_ref.shape[0]
    x_ref[...] = a_ref[...]

    def step(k, unused):
        current = x_ref[...]
        lanes = lax.broadcasted_iota(jnp.int32, (1, size), 1)
        rows = lax.broadcasted_iota(jnp.int32, (size, 1), 0)
        row = x_ref[pl.ds(k, 1), :]
        pivot = jnp.sum(jnp.where(lanes == k, row, 0.0), axis=1, keepdims=True)
        column = jnp.sum(jnp.where(lanes == k, current, 0.0), axis=1, keepdims=True)
        column = jnp.where(rows == k, 0.0, column)
        scaled = jnp.where(lanes == k, 1.0, row) / pivot
        updated = jnp.where(lanes == k, 0.0, current) - column * scaled
        x_ref[...] = jnp.where(rows == k, scaled, updated)
        return unused

    lax.fori_loop(0, size, step, 0)


def invert(a_refs, x_refs):
    size = a_refs[0].shape[0]
    for a_ref, x_ref in zip(a_refs, x_refs):
        a = a_ref[...]
        norm = jnp.max(jnp.sum(jnp.abs(a), axis=0, keepdims=True))
        scale = 1.8 / norm
        x_ref[...] = jnp.where(eye_mask(size), 2.0 * scale, 0.0) - (scale * scale) * a

    def low_step(unused_step, unused):
        for a_ref, x_ref in zip(a_refs, x_refs):
            x = x_ref[...]
            xb = x.astype(BF16)
            r = jnp.where(eye_mask(size), 1.0, 0.0) - dot(a_ref[...].astype(BF16), xb)
            x_ref[...] = x + dot(xb, r.astype(BF16))
        return unused

    lax.fori_loop(0, LOW_STEPS, low_step, 0)

    def high_step(state):
        step, unused = state
        worst = jnp.zeros((1, 1), F32)
        for a_ref, x_ref in zip(a_refs, x_refs):
            x = x_ref[...]
            xs = split(x)
            r = jnp.where(eye_mask(size), 1.0, 0.0) - dot3(split(a_ref[...]), xs)
            square = jnp.sum(jnp.sum(r * r, axis=0, keepdims=True), axis=1, keepdims=True)
            worst = jnp.where(square <= worst, worst, square)
            x_ref[...] = x + dot(xs[0], r.astype(BF16))
        return step + 1, worst[0, 0]

    def again(state):
        step, worst = state
        return jnp.logical_and(step < HIGH_STEPS, jnp.logical_not(worst < CONVERGED**2))

    unused, worst = lax.while_loop(again, high_step, (jnp.int32(0), jnp.float32(1.0)))

    @pl.when(jnp.logical_not(worst < CONVERGED**2))
    def _():
        for a_ref, x_ref in zip(a_refs, x_refs):
            gauss_jordan(a_ref, x_ref)


def factor_kernel(
    faces, rates, library, walls, ph_ref, pl_ref, gh_ref, gl_ref, schur, inverse
):
    count = rates.shape[0]
    half = count // 2
    size = library.shape[1]

    def block(i):
        row = library[pl.ds(rates[i], 1), :]
        return jnp.where(eye_mask(size), row, 0.0) + walls[faces[i]] + walls[faces[i + 1]]

    def keep(i, side, coupling):
        x = inverse[side]
        xs = split(x)
        ph_ref[i], pl_ref[i] = xs
        q = split(coupling)
        gs = split(dot3(xs, q))
        gh_ref[i], gl_ref[i] = gs
        return dot3(q, gs)

    schur[0] = block(0)
    schur[1] = block(count - 1)

    def level(i, unused):
        j = count - 1 - i
        invert([schur.at[0], schur.at[1]], [inverse.at[0], inverse.at[1]])
        schur[0] = block(i + 1) - keep(i, 0, walls[faces[i + 1]])
        schur[1] = block(j - 1) - keep(j, 1, walls[faces[j]])
        return unused

    lax.fori_loop(0, half - 1, level, 0)
    invert([schur.at[1]], [inverse.at[1]])
    schur[0] = schur[0] - keep(half, 1, walls[faces[half]])
    invert([schur.at[0]], [inverse.at[0]])
    xs = split(inverse[0])
    ph_ref[half - 1], pl_ref[half - 1] = xs


def residual_kernel(index, side, near, library, out):
    for e in range(side.shape[0]):
        total = side[e]
        for d in range(4):
            total = total - dot3(split(near[e, d]), split(library[index[e, d]]), True)
        out[e] = total


def sweep_kernel(own, residual, ph_ref, pl_ref, gh_ref, gl_ref, out, values):
    count = residual.shape[0]
    half = count // 2

    def pivots(i):
        return ph_ref[i], pl_ref[i]

    def steps(i):
        return gh_ref[i], gl_ref[i]

    carried = [None] * count
    low, high = residual[0], residual[count - 1]
    for i in range(half):
        j = count - 1 - i
        carried[i], carried[j] = split(low), split(high)
        if i + 1 < half:
            low = residual[i + 1] + dot3(carried[i], steps(i))
            high = residual[j - 1] + dot3(carried[j], steps(j))
    scaled = {i: dot3(carried[i], pivots(i)) for i in range(count) if i != half - 1}
    low = dot3(split(low + dot3(carried[half], steps(half))), pivots(half - 1))
    values[half - 1] = low
    lows = split(low)
    high = scaled[half] + dot3(lows, steps(half), True)
    values[half] = high
    highs = split(high)
    for i in range(half - 2, -1, -1):
        j = count - 1 - i
        low = scaled[i] + dot3(lows, steps(i), True)
        high = scaled[j] + dot3(highs, steps(j), True)
        values[i] = low
        values[j] = high
        lows, highs = split(low), split(high)
    mine = out.shape[0]
    for e in range(mine):
        out[e] = values[own[0] * mine + e]


def on_device(
    right_side,
    old_values,
    element_library,
    wall_library,
    face_library,
    element_index,
    wall_faces,
    face_index,
):
    size = wall_library.shape[1]
    vmem = pl.BlockSpec(memory_space=pltpu.VMEM)
    smem = pl.BlockSpec(memory_space=pltpu.SMEM)
    params = pltpu.CompilerParams(vmem_limit_bytes=48 * 1024 * 1024)
    own = old_values[0, 0]
    near = []
    for axis in ("span", "stream"):
        n = lax.axis_size(axis)
        up = lax.ppermute(own, axis, [(i, (i + 1) % n) for i in range(n)])
        near.append(up)
        near.append(
            up if n == 2 else lax.ppermute(own, axis, [((i + 1) % n, i) for i in range(n)])
        )
    near = jnp.stack(near, axis=1)
    rows = jnp.concatenate([element_index[0, 0][:, None], wall_faces[0, 0]], axis=1)
    rows = lax.all_gather(rows, "wall", axis=0, tiled=True)
    rates = rows[:, 0]
    faces = jnp.concatenate([rows[:, 1], rows[-1:, 2]])
    count = rows.shape[0]
    blocks = jax.ShapeDtypeStruct((count, size, size), BF16)
    factors = pl.pallas_call(
        factor_kernel,
        out_shape=[blocks] * 4,
        in_specs=[smem, smem, vmem, vmem],
        out_specs=[vmem] * 4,
        scratch_shapes=[pltpu.VMEM((2, size, size), F32), pltpu.VMEM((2, size, size), F32)],
        compiler_params=params,
        cost_estimate=pl.CostEstimate(
            flops=400 * 2 * size**3, bytes_accessed=count * 8 * size * size, transcendentals=0
        ),
        name="factor_line",
    )(faces, rates, element_library, wall_library)
    residual = pl.pallas_call(
        residual_kernel,
        out_shape=jax.ShapeDtypeStruct(own.shape, F32),
        in_specs=[smem, vmem, vmem, vmem],
        out_specs=vmem,
        compiler_params=params,
        name="residual",
    )(face_index[0, 0], right_side[0, 0], near, face_library)
    residual = lax.all_gather(residual, "wall", axis=0, tiled=True)
    place = jnp.reshape(lax.axis_index("wall"), (1,)).astype(jnp.int32)
    new_values = pl.pallas_call(
        sweep_kernel,
        out_shape=jax.ShapeDtypeStruct(own.shape, F32),
        in_specs=[smem] + [vmem] * 5,
        out_specs=vmem,
        scratch_shapes=[pltpu.VMEM((count,) + own.shape[1:], F32)],
        compiler_params=params,
        name="sweep",
    )(place, residual, *factors)
    return new_values[None, None]


def solution(mesh):
    placed = (
        P("span", "stream", "wall", None, None),
        P("span", "stream", "wall", None, None),
        P(),
        P(),
        P(),
        P("span", "stream", "wall"),
        P("span", "stream", "wall", None),
        P("span", "stream", "wall", None),
    )
    return jax.shard_map(
        on_device,
        mesh=mesh,
        in_specs=placed,
        out_specs=P("span", "stream", "wall", None, None),
        check_vma=False,
    )
```

time: 779 us -> 81.5 us (0.10); the launches traced: 771 us -> 81.2 us
  other arithmetic: 486 us -> 1.54 us
  matrix products: 127 us -> 0 us
  local copies, waits for them, and re-layouts: 81 us -> 6.16 us
  Pallas kernels: 0 us -> 53 us
  between operations: 32.4 us -> 0.08 us
  waiting for transfers between devices: 21 us -> 0.01 us
    another operation x87 -> x1, other arithmetic: 478 us -> 0.06 us  [on_device(): near = jnp.stack(near, axis=1)]
    another operation x125 -> x0, matrix products: 87.3 us -> none  [the longest x75 52.4 us: lower_solve(): return jax.scipy.linalg.solve_triangular(factor, values, lower=True)]
    pallas_call x0 -> x3, Pallas kernels: none -> 53 us  [the longest x1 43.1 us: on_device(): pl.pallas_call(factor_kernel, out_shape=[blocks] * 4, in_specs=[smem, sme...]
    another operation x69 -> x1, local copies, waits for them, and re-layouts: 41.9 us -> 0.74 us  [on_device(): element_index[0, 0][:, None]]
    dot_general x24 -> x0, matrix products: 39.7 us -> none  [the longest x3 7.59 us: substructure(): jnp.dot(scaled.T, scaled, precision=HIGHEST)]
    ppermute x4 -> x3, waiting for transfers between devices: 20.9 us -> 0.01 us  [the longest x2 0.01 us: on_device(): up = lax.ppermute(own, axis, [(i, (i + 1) % n) for i in range(n)])]
    unnamed x121 -> x18, local copies, waits for them, and re-layouts: 20.2 us -> 4.67 us
  transfers between devices with their start and end apart: 7 -> 3, of which waited for: 2 -> 0; matrix products, arithmetic and copies ran while one was open for 36% -> 4% of each run, Pallas kernels for 0% -> 53%
where the time goes in v1:
time: 81.5 us; the launch traced here: 81.2 us
  Pallas kernels  53 us (65%)
  blocking collectives  13.9 us (17%)
  starting transfers between devices  6.57 us (8%)
  local copies, waits for them, and re-layouts  6.16 us (8%)
  other arithmetic  1.54 us (2%)
    pallas_call x1, Pallas kernels, on_device(): pl.pallas_call(factor_kernel, out_shape=[blocks] * 4, in_specs=[smem, sme...  43.1 us
    all_gather x1, blocking collectives, on_device(): residual = lax.all_gather(residual, 'wall', axis=0, tiled=True)  8.87 us
    pallas_call x1, Pallas kernels, on_device(): pl.pallas_call(sweep_kernel, out_shape=jax.ShapeDtypeStruct(own.shape, F3...  7.36 us
    all_gather x1, blocking collectives, on_device(): rows = lax.all_gather(rows, 'wall', axis=0, tiled=True)  5.06 us
    unnamed x18, local copies, waits for them, and re-layouts  4.67 us
    ppermute x1, starting transfers between devices, on_device(): lax.ppermute(own, axis, [((i + 1) % n, i) for i in range(n)])  3.6 us
    ppermute x2, starting transfers between devices, on_device(): up = lax.ppermute(own, axis, [(i, (i + 1) % n) for i in range(n)])  2.97 us
    pallas_call x1, Pallas kernels, on_device(): pl.pallas_call(residual_kernel, out_shape=jax.ShapeDtypeStruct(own.shape,...  2.5 us
  transfers between devices with their start and end apart: 3, of which 0 were waited for; matrix products, arithmetic and copies ran while one was open for 4% of the time, Pallas kernels for 53%

profile of v1, /device:TPU:0, one launch (start us, length us, event | category | flops | bytes accessed | tf_op | source)
XLA Modules:
  0.0 81.2 jit_solution(14782511039888800262)
XLA Ops:
  0.0 3.0 %collective-permute-start.2 = (f32[2,64,320]{2,1,0:T(8,128)}, f32[2,64,320]{2,1,0:T(8,128)S(1)}, u32[]{:S(2)}, u32[]{:S(2)}) collective-permute-start(f32[2,64,320]{2,1,0:T(8,128)} %bitcast.26), channel_id=1, source_target_pairs={{0,1},{1,0},{2,3},{3,2},{4,5},{5,4},{6,7},{7,6},{8,9},{9,8},{10,11... | collective-permute-start | bytes 491528 | tf_op jit(solution)/shard_map/ppermute | solution.py:201
  3.0 3.6 %collective-permute-start.1 = (f32[2,64,320]{2,1,0:T(8,128)}, f32[2,64,320]{2,1,0:T(8,128)S(1)}, u32[]{:S(2)}, u32[]{:S(2)}) collective-permute-start(f32[2,64,320]{2,1,0:T(8,128)} %bitcast.27), channel_id=1, source_target_pairs={{2,0},{4,2},{6,4},{0,6},{3,1},{5,3},{7,5},{1,7},{10,8},{12,10},{14... | collective-permute-start | bytes 491528 | tf_op jit(solution)/shard_map/ppermute | solution.py:204
  6.6 0.7 copy.17
  7.3 0.8 add_bitcast_fusion
  8.1 0.0 collective-permute-start
  8.1 5.1 %all-gather = s32[4,2,3]{2,1,0:T(2,128)S(1)} all-gather(s32[1,2,3]{2,1,0:T(2,128)S(1)} %add_bitcast_fusion), channel_id=1, replica_groups=mesh['wall'=4,'span'=4,'stream'=2] {'wall'}, dimensions={0}, use_global_device_ids=true | all-gather | bytes 120 | tf_op jit(solution)/shard_map/all_gather | solution.py:208
  13.1 0.6 slice.10
  13.7 0.2 slice_reduce_fusion
  13.9 0.7 pad_add_fusion.faces
  14.6 1.4 %copy-done.7 = f32[3,320,320]{2,1,0:T(8,128)S(1)} copy-done((f32[3,320,320]{2,1,0:T(8,128)S(1)}, f32[3,320,320]{2,1,0:T(8,128)}, u32[]{:S(2)}) %copy-start.7) | copy-done | bytes 1228824
  16.0 0.7 copy-done.8
  16.7 43.1 %factor_line.1 = (bf16[8,320,320]{2,1,0:T(8,128)(2,1)S(1)}, bf16[8,320,320]{2,1,0:T(8,128)(2,1)S(1)}, bf16[8,320,320]{2,1,0:T(8,128)(2,1)}, bf16[8,320,320]{2,1,0:T(8,128)(2,1)}) custom-call(s32[9]{0:T(128)S(1)} %pad_add_fusion.faces, s32[8]{0:T(128)S(1)} %get-tuple-element.13.rates, f32[8,320]{1,0:T(8,128)S(1)} %copy-done.8, f32[3,320,320]{2,1,0:T(8,128)S(1)} %copy-done.7), custom_call_target="tpu_custom_call" | custom-call | flops 26214400000 | bytes 6553600 | tf_op jit(solution)/shard_map/factor_line/pallas_call | solution.py:213
  59.8 1.3 %copy-done.1 = bf16[8,320,320]{2,1,0:T(8,128)(2,1)} copy-done((bf16[8,320,320]{2,1,0:T(8,128)(2,1)}, bf16[8,320,320]{2,1,0:T(8,128)(2,1)S(1)}, u32[]{:S(2)}) %copy-start.1) | copy-done | bytes 1638424
  61.1 1.3 %copy-done.3 = bf16[8,320,320]{2,1,0:T(8,128)(2,1)} copy-done((bf16[8,320,320]{2,1,0:T(8,128)(2,1)}, bf16[8,320,320]{2,1,0:T(8,128)(2,1)S(1)}, u32[]{:S(2)}) %copy-start.3) | copy-done | bytes 1638424
  62.4 0.0 collective-permute-done.2
  62.4 0.0 collective-permute-done.1
  62.4 0.0 collective-permute-done
  62.4 0.1 pad_maximum_fusion.near
  62.5 0.0 copy-done
  62.5 0.0 copy-done.5
  62.5 0.0 copy-done.6
  62.5 2.5 %residual.1 = f32[2,64,320]{2,1,0:T(8,128)S(1)} custom-call(s32[2,4]{1,0:T(2,128)S(1)} %bitcast.19, f32[2,64,320]{2,1,0:T(8,128)S(1)} %bitcast.18, f32[2,4,64,320]{3,2,1,0:T(8,128)S(1)} %pad_maximum_fusion.near, f32[4,320,320]{2,1,0:T(8,128)S(1)} %copy-done), custom_call_target="tpu_custom_call" | custom-call | tf_op jit(solution)/shard_map/residual/pallas_call | solution.py:225
  65.0 8.9 %all_gather.6.residual = f32[8,64,320]{2,1,0:T(8,128)S(1)} all-gather(f32[2,64,320]{2,1,0:T(8,128)S(1)} %residual.1), channel_id=1, replica_groups=mesh['wall'=4,'span'=4,'stream'=2] {'wall'}, dimensions={0}, use_global_device_ids=true | all-gather | bytes 819200 | tf_op jit(solution)/shard_map/all_gather | solution.py:233
  73.9 7.4 %sweep.1 = f32[2,64,320]{2,1,0:T(8,128)} custom-call(s32[1]{0:T(128)} %bitcast.own, f32[8,64,320]{2,1,0:T(8,128)S(1)} %all_gather.6.residual, bf16[8,320,320]{2,1,0:T(8,128)(2,1)S(1)} %copy-done.2, bf16[8,320,320]{2,1,0:T(8,128)(2,1)S(1)} %copy-done.4, bf16[8,320,320]{2,1,0:T(8,128)(2,1)} %get-tuple-element.11.gh_ref, ...), custom_call_target="tpu_custom_call" | custom-call | tf_op jit(solution)/shard_map/sweep/pallas_call | solution.py:235
  (11 shorter events, 0.0 us)
Async XLA Ops:
  0.0 62.4 %collective-permute-start.2 = (f32[2,64,320]{2,1,0:T(8,128)}, f32[2,64,320]{2,1,0:T(8,128)S(1)}, u32[]{:S(2)}, u32[]{:S(2)}) collective-permute-start(f32[2,64,320]{2,1,0:T(8,128)} %bitcast.26), channel_id=1, source_target_pairs={{0,1},{1,0},{2,3},{3,2},{4,5},{5,4},{6,7},{7,6},{8,9},{9,8},{10,11... | collective-permute-start | bytes 491528 | tf_op jit(solution)/shard_map/ppermute | solution.py:201
  3.0 59.4 %collective-permute-start.1 = (f32[2,64,320]{2,1,0:T(8,128)}, f32[2,64,320]{2,1,0:T(8,128)S(1)}, u32[]{:S(2)}, u32[]{:S(2)}) collective-permute-start(f32[2,64,320]{2,1,0:T(8,128)} %bitcast.27), channel_id=1, source_target_pairs={{2,0},{4,2},{6,4},{0,6},{3,1},{5,3},{7,5},{1,7},{10,8},{12,10},{14... | collective-permute-start | bytes 491528 | tf_op jit(solution)/shard_map/ppermute | solution.py:204
  8.1 54.3 %collective-permute-start = (f32[2,64,320]{2,1,0:T(8,128)}, f32[2,64,320]{2,1,0:T(8,128)S(1)}, u32[]{:S(2)}, u32[]{:S(2)}) collective-permute-start(f32[2,64,320]{2,1,0:T(8,128)} %bitcast.28), channel_id=1, source_target_pairs={{0,2},{2,4},{4,6},{6,0},{1,3},{3,5},{5,7},{7,1},{8,10},{10,12},{12... | collective-permute-start | bytes 491528 | tf_op jit(solution)/shard_map/ppermute | solution.py:201
  14.6 1.4 %copy-start.7 = (f32[3,320,320]{2,1,0:T(8,128)S(1)}, f32[3,320,320]{2,1,0:T(8,128)}, u32[]{:S(2)}) copy-start(f32[3,320,320]{2,1,0:T(8,128)} %walls.1) | copy-start | bytes 3686404
  16.0 0.7 copy-start.8
  16.7 45.8 %copy-start = (f32[4,320,320]{2,1,0:T(8,128)S(1)}, f32[4,320,320]{2,1,0:T(8,128)}, u32[]{:S(2)}) copy-start(f32[4,320,320]{2,1,0:T(8,128)} %library.2) | copy-start | bytes 4915204
  16.7 45.8 %copy-start.5 = (f32[1,1,2,64,320]{4,3,2,1,0:T(8,128)S(1)}, f32[1,1,2,64,320]{4,3,2,1,0:T(8,128)}, u32[]{:S(2)}) copy-start(f32[1,1,2,64,320]{4,3,2,1,0:T(8,128)} %param.8) | copy-start | bytes 491524
  16.7 45.8 %copy-start.6 = (s32[1,1,2,4]{3,2,1,0:T(2,128)S(1)}, s32[1,1,2,4]{3,2,1,0:T(2,128)}, u32[]{:S(2)}) copy-start(s32[1,1,2,4]{3,2,1,0:T(2,128)} %param.15) | copy-start | bytes 100
  59.8 1.3 %copy-start.1 = (bf16[8,320,320]{2,1,0:T(8,128)(2,1)}, bf16[8,320,320]{2,1,0:T(8,128)(2,1)S(1)}, u32[]{:S(2)}) copy-start(bf16[8,320,320]{2,1,0:T(8,128)(2,1)S(1)} %get-tuple-element.9.ph_ref) | copy-start | bytes 4915204
  61.1 1.3 %copy-start.3 = (bf16[8,320,320]{2,1,0:T(8,128)(2,1)}, bf16[8,320,320]{2,1,0:T(8,128)(2,1)S(1)}, u32[]{:S(2)}) copy-start(bf16[8,320,320]{2,1,0:T(8,128)(2,1)S(1)} %get-tuple-element.10.pl_ref) | copy-start | bytes 4915204
  62.5 11.4 %copy-start.2 = (bf16[8,320,320]{2,1,0:T(8,128)(2,1)S(1)}, bf16[8,320,320]{2,1,0:T(8,128)(2,1)}, u32[]{:S(2)}) copy-start(bf16[8,320,320]{2,1,0:T(8,128)(2,1)} %copy-done.1) | copy-start | bytes 4915204
  62.5 11.4 %copy-start.4 = (bf16[8,320,320]{2,1,0:T(8,128)(2,1)S(1)}, bf16[8,320,320]{2,1,0:T(8,128)(2,1)}, u32[]{:S(2)}) copy-start(bf16[8,320,320]{2,1,0:T(8,128)(2,1)} %copy-done.3) | copy-start | bytes 4915204

commit v2 on v1

v2 whole, which is shorter than its diff:
```python
import functools
import jax
import jax.numpy as jnp
from jax import lax
from jax.experimental import pallas as pl
from jax.experimental.pallas import tpu as pltpu
from jax.sharding import PartitionSpec as P

F32 = jnp.float32
BF16 = jnp.bfloat16
LOW_STEPS = 2
HIGH_STEPS = 4
CONVERGED = 0.08


def dot(a, b, transposed=False):
    dims = (((1,), (1,)), ((), ())) if transposed else (((1,), (0,)), ((), ()))
    return lax.dot_general(a, b, dims, preferred_element_type=F32)


def split(a):
    high = a.astype(BF16)
    return high, (a - high.astype(F32)).astype(BF16)


def dot3(a, b, transposed=False):
    return (
        dot(a[0], b[0], transposed) + (dot(a[0], b[1], transposed) + dot(a[1], b[0], transposed))
    )


def eye_mask(size):
    row = lax.broadcasted_iota(jnp.int32, (size, size), 0)
    col = lax.broadcasted_iota(jnp.int32, (size, size), 1)
    return row == col


def gauss_jordan(a_ref, x_ref):
    size = a_ref.shape[0]
    x_ref[...] = a_ref[...]

    def step(k, unused):
        current = x_ref[...]
        lanes = lax.broadcasted_iota(jnp.int32, (1, size), 1)
        rows = lax.broadcasted_iota(jnp.int32, (size, 1), 0)
        row = x_ref[pl.ds(k, 1), :]
        pivot = jnp.sum(jnp.where(lanes == k, row, 0.0), axis=1, keepdims=True)
        column = jnp.sum(jnp.where(lanes == k, current, 0.0), axis=1, keepdims=True)
        column = jnp.where(rows == k, 0.0, column)
        scaled = jnp.where(lanes == k, 1.0, row) / pivot
        updated = jnp.where(lanes == k, 0.0, current) - column * scaled
        x_ref[...] = jnp.where(rows == k, scaled, updated)
        return unused

    lax.fori_loop(0, size, step, 0)


def refine(a_ref, x_ref):
    x = x_ref[...]
    xs = split(x)
    r = jnp.where(eye_mask(x.shape[0]), 1.0, 0.0) - dot3(split(a_ref[...]), xs)
    rb = r.astype(BF16)
    x_ref[...] = x + dot(xs[0], (r + dot(rb, rb)).astype(BF16))
    return jnp.sum(jnp.sum(r * r, axis=0, keepdims=True), axis=1, keepdims=True)


def invert(a_refs, x_refs):
    size = a_refs[0].shape[0]
    pairs = list(zip(a_refs, x_refs))
    mask = eye_mask(size)
    lows, xs = [], []
    for a_ref, unused in pairs:
        a = a_ref[...]
        trace = jnp.sum(jnp.sum(jnp.where(mask, a, 0.0), axis=0, keepdims=True), axis=1, keepdims=True)
        square = jnp.sum(jnp.sum(a * a, axis=0, keepdims=True), axis=1, keepdims=True)
        scale = trace / square
        xs.append(jnp.where(mask, 2.0 * scale, 0.0) - (scale * scale) * a)
        lows.append(a.astype(BF16))
    for step in range(LOW_STEPS):
        xbs = [x.astype(BF16) for x in xs]
        rs = [jnp.where(mask, 1.0, 0.0) - dot(low, xb) for low, xb in zip(lows, xbs)]
        xs = [x + dot(xb, r.astype(BF16)) for x, xb, r in zip(xs, xbs, rs)]
    for (unused, x_ref), x in zip(pairs, xs):
        x_ref[...] = x
    worst = sum(refine(a_ref, x_ref) for a_ref, x_ref in pairs)[0, 0]

    @pl.when(jnp.logical_not(worst < CONVERGED**2))
    def _():
        def again(state):
            step, now = state
            return jnp.logical_and(step < HIGH_STEPS, jnp.logical_not(now < CONVERGED**2))

        def more(state):
            return state[0] + 1, sum(refine(*pair) for pair in pairs)[0, 0]

        unused, last = lax.while_loop(again, more, (jnp.int32(0), worst))

        @pl.when(jnp.logical_not(last < CONVERGED**2))
        def _():
            for pair in pairs:
                gauss_jordan(*pair)


class Line:
    def __init__(self, rows, library, walls, table):
        self.library, self.walls, self.table = library, walls, table
        count = len(rows)
        mine = rows[0].shape[0]
        place = lax.axis_index("wall")
        for shift, ref in enumerate(rows):
            owner = lax.rem(place - shift + count, count)
            for e in range(mine):
                for c in range(3):
                    table[owner * mine + e, c] = ref[e, c]
        self.count = count * mine
        self.size = walls.shape[1]

    def face(self, i):
        if i == self.count:
            return self.walls[self.table[i - 1, 2]]
        return self.walls[self.table[i, 1]]

    def block(self, i):
        row = self.library[pl.ds(self.table[i, 0], 1), :]
        return jnp.where(eye_mask(self.size), row, 0.0) + self.face(i) + self.face(i + 1)


def keep(x_ref, coupling, stores, slot):
    xs = split(x_ref[...])
    q = split(coupling)
    gs = split(dot3(xs, q))
    for store, value in zip(stores, xs + gs):
        store[slot] = value
    return dot3(q, gs)


def levels_kernel(first, last, wall_count, with_middle, *refs):
    rows, (library, walls) = refs[:wall_count], refs[wall_count : wall_count + 2]
    refs = refs[wall_count + 2 :]
    before = refs[0] if first > 0 else None
    refs = refs[1:] if first > 0 else refs
    schur, stores, (inverse, table) = refs[0], refs[1:5], refs[5:]
    line = Line(rows, library, walls, table)
    top = line.count - 1
    if first > 0:
        schur[...] = before[...]
    else:
        schur[0] = line.block(0)
        schur[1] = line.block(top)
    for i in range(first, last):
        slot = 2 * (i - first)
        invert([schur.at[0], schur.at[1]], [inverse.at[0], inverse.at[1]])
        low = keep(inverse.at[0], line.face(i + 1), stores, slot)
        high = keep(inverse.at[1], line.face(top - i), stores, slot + 1)
        schur[0] = line.block(i + 1) - low
        schur[1] = line.block(top - i - 1) - high
    if with_middle:
        invert([schur.at[1]], [inverse.at[1]])
        schur[0] = schur[0] - keep(
            inverse.at[1], line.face(line.count // 2), stores, 2 * (last - first)
        )


def residual_kernel(index, side, near_0, near_1, near_2, near_3, library, out):
    near = (near_0, near_1, near_2, near_3)
    for e in range(side.shape[0]):
        total = side[e]
        for d in range(4):
            total = total - dot3(split(near[d][e]), split(library[index[e, d]]), True)
        out[e] = total


def sweep_kernel(wall_count, split_level, *refs):
    sides, refs = refs[:wall_count], refs[wall_count:]
    schur, early, late, (out, residual, values, inverse) = refs[0], refs[1:5], refs[5:9], refs[9:]
    mine = out.shape[0]
    place = lax.axis_index("wall")
    for shift, ref in enumerate(sides):
        owner = lax.rem(place - shift + wall_count, wall_count)
        for e in range(mine):
            residual[owner * mine + e] = ref[e]
    count = wall_count * mine
    half = count // 2

    def part(i, which):
        level = i if i < half else count - 1 - i
        side = 0 if i < half else 1
        store, base = (early, 0) if level < split_level else (late, split_level)
        slot = 2 * (level - base) + (side if level < half - 1 else 0)
        return store[2 * which][slot], store[2 * which + 1][slot]

    invert([schur.at[0]], [inverse])
    carried = [None] * count
    low, high = residual[0], residual[count - 1]
    for i in range(half):
        j = count - 1 - i
        carried[i], carried[j] = split(low), split(high)
        if i + 1 < half:
            low = residual[i + 1] + dot3(carried[i], part(i, 1))
            high = residual[j - 1] + dot3(carried[j], part(j, 1))
    scaled = {i: dot3(carried[i], part(i, 0)) for i in range(count) if i != half - 1}
    low = low + dot3(carried[half], part(half, 1))
    low = dot3(split(low), split(inverse[...]))
    values[half - 1] = low
    lows = split(low)
    high = scaled[half] + dot3(lows, part(half, 1), True)
    values[half] = high
    highs = split(high)
    for i in range(half - 2, -1, -1):
        j = count - 1 - i
        low = scaled[i] + dot3(lows, part(i, 1), True)
        high = scaled[j] + dot3(highs, part(j, 1), True)
        values[i] = low
        values[j] = high
        lows, highs = split(low), split(high)
    for e in range(mine):
        out[e] = values[place * mine + e]


def on_device(
    right_side,
    old_values,
    element_library,
    wall_library,
    face_library,
    element_index,
    wall_faces,
    face_index,
):
    size = wall_library.shape[1]
    vmem = pl.BlockSpec(memory_space=pltpu.VMEM)
    smem = pl.BlockSpec(memory_space=pltpu.SMEM)
    params = pltpu.CompilerParams(vmem_limit_bytes=28 * 1024 * 1024)
    wall_count = lax.axis_size("wall")
    own = old_values[0, 0]
    mine = own.shape[0]
    count = wall_count * mine
    half = count // 2

    def shifted(array, axis, shift):
        n = lax.axis_size(axis)
        return lax.ppermute(array, axis, [(i, (i + shift) % n) for i in range(n)])

    rows = jnp.concatenate([element_index[0, 0][:, None], wall_faces[0, 0]], axis=1)
    rows = [rows] + [shifted(rows, "wall", s) for s in range(1, wall_count)]
    near = []
    for axis in ("span", "stream"):
        up = shifted(own, axis, 1)
        near += [up, up if lax.axis_size(axis) == 2 else shifted(own, axis, -1)]

    def factor(first, last, with_middle, schur, name):
        slots = 2 * (last - first) + int(with_middle)
        blocks = jax.ShapeDtypeStruct((slots, size, size), BF16)
        return pl.pallas_call(
            functools.partial(levels_kernel, first, last, wall_count, with_middle),
            out_shape=[jax.ShapeDtypeStruct((2, size, size), F32)] + [blocks] * 4,
            in_specs=[smem] * wall_count + [vmem] * (2 + len(schur)),
            out_specs=[vmem] * 5,
            scratch_shapes=[pltpu.VMEM((2, size, size), F32), pltpu.SMEM((count, 3), jnp.int32)],
            compiler_params=params,
            cost_estimate=pl.CostEstimate(
                flops=slots * 160 * size**3, bytes_accessed=16 * size * size, transcendentals=0
            ),
            name=name,
        )(*rows, element_library, wall_library, *schur)

    cut = max(1, half - 2)
    schur, *early = factor(0, cut, False, [], "factor_outer")
    schur, *near = lax.optimization_barrier((schur, *near))
    residual = pl.pallas_call(
        residual_kernel,
        out_shape=jax.ShapeDtypeStruct(own.shape, F32),
        in_specs=[smem] + [vmem] * 6,
        out_specs=vmem,
        compiler_params=params,
        name="residual",
    )(face_index[0, 0], right_side[0, 0], *near, face_library)
    schur, residual = lax.optimization_barrier((schur, residual))
    sides = [residual] + [shifted(residual, "wall", s) for s in range(1, wall_count)]
    schur, *late = factor(cut, half - 1, True, [schur], "factor_inner")
    new_values = pl.pallas_call(
        functools.partial(sweep_kernel, wall_count, cut),
        out_shape=jax.ShapeDtypeStruct(own.shape, F32),
        in_specs=[vmem] * (wall_count + 9),
        out_specs=vmem,
        scratch_shapes=[
            pltpu.VMEM((count,) + own.shape[1:], F32),
            pltpu.VMEM((count,) + own.shape[1:], F32),
            pltpu.VMEM((size, size), F32),
        ],
        compiler_params=params,
        name="sweep",
    )(*sides, schur, *early, *late)
    return new_values[None, None]


def solution(mesh):
    placed = (
        P("span", "stream", "wall", None, None),
        P("span", "stream", "wall", None, None),
        P(),
        P(),
        P(),
        P("span", "stream", "wall"),
        P("span", "stream", "wall", None),
        P("span", "stream", "wall", None),
    )
    return jax.shard_map(
        on_device,
        mesh=mesh,
        in_specs=placed,
        out_specs=P("span", "stream", "wall", None, None),
        check_vma=False,
    )
```

time: 81.5 us -> 109 us (1.34)
  Pallas kernels: 53 us -> 92.6 us
  blocking collectives: 13.9 us -> 0 us
  starting transfers between devices: 6.57 us -> 11.8 us
  local copies, waits for them, and re-layouts: 6.16 us -> 2.83 us
    pallas_call x2 -> x3, Pallas kernels: 50.5 us -> 90.1 us  [the longest x1 62.8 us: on_device(): pl.pallas_call(functools.partial(sweep_kernel, wall_count, cut), out_shap...]
    all_gather x2 -> x0, blocking collectives: 13.9 us -> none  [the longest x1 8.87 us: on_device(): residual = lax.all_gather(residual, 'wall', axis=0, tiled=True)]
    ppermute x3 -> x9, starting transfers between devices: 6.57 us -> 11.8 us  [shifted(): return lax.ppermute(array, axis, [(i, (i + shift) % n) for i in range(n)])]
    unnamed x18 -> x10, local copies, waits for them, and re-layouts: 4.67 us -> 2.09 us
  transfers between devices with their start and end apart: 3 -> 9, of which waited for: 0 -> 0; matrix products, arithmetic and copies ran while one was open for 4% -> 0% of each run, Pallas kernels for 53% -> 25%
where the time goes in v2:
time: 109 us; the launch traced here: 108 us
  Pallas kernels  92.6 us (85%)
  starting transfers between devices  11.8 us (11%)
  local copies, waits for them, and re-layouts  2.83 us (3%)
    pallas_call x1, Pallas kernels, on_device(): pl.pallas_call(functools.partial(sweep_kernel, wall_count, cut), out_shap...  62.8 us
    pallas_call x2, Pallas kernels, factor(): pl.pallas_call(functools.partial(levels_kernel, first, last, wall_count,...  27.3 us
    ppermute x9, starting transfers between devices, shifted(): return lax.ppermute(array, axis, [(i, (i + shift) % n) for i in range(n)])  11.8 us
    pallas_call x1, Pallas kernels, on_device(): pl.pallas_call(residual_kernel, out_shape=jax.ShapeDtypeStruct(own.shape,...  2.52 us
  transfers between devices with their start and end apart: 9, of which 0 were waited for; matrix products, arithmetic and copies ran while one was open for 0% of the time, Pallas kernels for 25%

profile of v2, /device:TPU:0, one launch (start us, length us, event | category | flops | bytes accessed | tf_op | source)
XLA Modules:
  0.0 108.1 jit_solution(969692055378289643)
XLA Ops:
  0.0 0.7 copy.9
  0.7 0.8 pad_add_fusion.refs_0_
  1.5 0.5 collective-permute-start
  1.9 2.5 %collective-permute-start.1 = (s32[2,3]{1,0:T(2,128)S(1)}, s32[2,3]{1,0:T(2,128)S(1)}, u32[]{:S(2)}, u32[]{:S(2)}) collective-permute-start(s32[2,3]{1,0:T(2,128)S(1)} %pad_add_fusion.refs_0_), channel_id=1, source_target_pairs={{0,16},{8,24},{16,0},{24,8},{1,17},{9,25},{17,1},{25,9},{2,18},{10... | collective-permute-start | bytes 80 | tf_op jit(solution)/shard_map/ppermute | solution.py:242
  4.5 1.4 %collective-permute-start.2 = (s32[2,3]{1,0:T(2,128)S(1)}, s32[2,3]{1,0:T(2,128)S(1)}, u32[]{:S(2)}, u32[]{:S(2)}) collective-permute-start(s32[2,3]{1,0:T(2,128)S(1)} %pad_add_fusion.refs_0_), channel_id=1, source_target_pairs={{0,24},{8,0},{16,8},{24,16},{1,25},{9,1},{17,9},{25,17},{2,26},{10... | collective-permute-start | bytes 80 | tf_op jit(solution)/shard_map/ppermute | solution.py:242
  5.9 1.6 %collective-permute-start.3 = (f32[2,64,320]{2,1,0:T(8,128)}, f32[2,64,320]{2,1,0:T(8,128)S(1)}, u32[]{:S(2)}, u32[]{:S(2)}) collective-permute-start(f32[2,64,320]{2,1,0:T(8,128)} %bitcast.9), channel_id=1, source_target_pairs={{0,2},{2,4},{4,6},{6,0},{1,3},{3,5},{5,7},{7,1},{8,10},{10,12},{12... | collective-permute-start | bytes 491528 | tf_op jit(solution)/shard_map/ppermute | solution.py:242
  7.5 2.2 %collective-permute-start.4 = (f32[2,64,320]{2,1,0:T(8,128)}, f32[2,64,320]{2,1,0:T(8,128)S(1)}, u32[]{:S(2)}, u32[]{:S(2)}) collective-permute-start(f32[2,64,320]{2,1,0:T(8,128)} %bitcast.10), channel_id=1, source_target_pairs={{0,6},{2,0},{4,2},{6,4},{1,7},{3,1},{5,3},{7,5},{8,14},{10,8},{12,... | collective-permute-start | bytes 491528 | tf_op jit(solution)/shard_map/ppermute | solution.py:242
  9.7 0.0 collective-permute-done.refs_1_
  9.7 1.5 %collective-permute-start.5 = (f32[2,64,320]{2,1,0:T(8,128)}, f32[2,64,320]{2,1,0:T(8,128)S(1)}, u32[]{:S(2)}, u32[]{:S(2)}) collective-permute-start(f32[2,64,320]{2,1,0:T(8,128)} %bitcast.11), channel_id=1, source_target_pairs={{0,1},{1,0},{2,3},{3,2},{4,5},{5,4},{6,7},{7,6},{8,9},{9,8},{10,11... | collective-permute-start | bytes 491528 | tf_op jit(solution)/shard_map/ppermute | solution.py:242
  11.3 0.0 collective-permute-done.1.refs_2_
  11.3 0.0 collective-permute-done.2.refs_3_
  11.3 1.4 %copy-done.3 = f32[3,320,320]{2,1,0:T(8,128)S(1)} copy-done((f32[3,320,320]{2,1,0:T(8,128)S(1)}, f32[3,320,320]{2,1,0:T(8,128)}, u32[]{:S(2)}) %copy-start.3) | copy-done | bytes 1228824
  12.6 0.7 copy-done.4
  13.3 12.9 %factor_outer.1 = (f32[2,320,320]{2,1,0:T(8,128)S(1)}, bf16[4,320,320]{2,1,0:T(8,128)(2,1)S(1)}, bf16[4,320,320]{2,1,0:T(8,128)(2,1)S(1)}, bf16[4,320,320]{2,1,0:T(8,128)(2,1)S(1)}, bf16[4,320,320]{2,1,0:T(8,128)(2,1)S(1)}) custom-call(s32[2,3]{1,0:T(2,128)S(1)} %pad_add_fusion.refs_0_, s32[2,3]{1,0:T(2,128)S(1)} %collective-permute-done.refs_1_, ...), custom_call_target="tpu_custom_call" | custom-call | flops 20971520000 | bytes 1638400 | tf_op jit(solution)/shard_map/factor_outer/pallas_call | solution.py:254
  26.3 0.0 collective-permute-done.3.near_0
  26.3 0.0 collective-permute-done.4.near_1
  26.3 2.5 %residual.1.refs_0_ = f32[2,64,320]{2,1,0:T(8,128)S(1)} custom-call(s32[2,4]{1,0:T(2,128)S(1)} %bitcast.7, f32[2,64,320]{2,1,0:T(8,128)S(1)} %bitcast.6, f32[2,64,320]{2,1,0:T(8,128)S(1)} %collective-permute-done.3.near_0, f32[2,64,320]{2,1,0:T(8,128)S(1)} %collective-permute-done.4.near_1, f32[2,64,320]{2,1,0:T(8,128)S(1)} %collective-permute-done.5.near_2.near_3, ...), custom_call_target="tpu_custom_call" | custom-call | tf_op jit(solution)/shard_map/residual/pallas_call | solution.py:270
  28.8 0.1 collective-permute-start.6
  28.9 0.6 collective-permute-start.7
  29.5 1.4 %collective-permute-start.8 = (f32[2,64,320]{2,1,0:T(8,128)S(1)}, f32[2,64,320]{2,1,0:T(8,128)S(1)}, u32[]{:S(2)}, u32[]{:S(2)}) collective-permute-start(f32[2,64,320]{2,1,0:T(8,128)S(1)} %residual.1.refs_0_), channel_id=1, source_target_pairs={{0,24},{8,0},{16,8},{24,16},{1,25},{9,1},{17,9},{25,17},{2,26},{10... | collective-permute-start | bytes 491528 | tf_op jit(solution)/shard_map/ppermute | solution.py:242
  30.9 14.4 %factor_inner.1 = (f32[2,320,320]{2,1,0:T(8,128)S(1)}, bf16[3,320,320]{2,1,0:T(8,128)(2,1)S(1)}, bf16[3,320,320]{2,1,0:T(8,128)(2,1)S(1)}, bf16[3,320,320]{2,1,0:T(8,128)(2,1)S(1)}, bf16[3,320,320]{2,1,0:T(8,128)(2,1)S(1)}) custom-call(s32[2,3]{1,0:T(2,128)S(1)} %pad_add_fusion.refs_0_, s32[2,3]{1,0:T(2,128)S(1)} %collective-permute-done.refs_1_, ...), custom_call_target="tpu_custom_call" | custom-call | flops 15728640000 | bytes 1638400 | tf_op jit(solution)/shard_map/factor_inner/pallas_call | solution.py:254
  45.3 0.0 collective-permute-done.6.refs_1_
  45.3 0.0 collective-permute-done.7.refs_2_
  45.3 62.8 %sweep.1 = f32[2,64,320]{2,1,0:T(8,128)} custom-call(f32[2,64,320]{2,1,0:T(8,128)S(1)} %residual.1.refs_0_, f32[2,64,320]{2,1,0:T(8,128)S(1)} %collective-permute-done.6.refs_1_, f32[2,64,320]{2,1,0:T(8,128)S(1)} %collective-permute-done.7.refs_2_, f32[2,64,320]{2,1,0:T(8,128)S(1)} %collective-permute-done.8.refs_3_, ...), custom_call_target="tpu_custom_call" | custom-call | tf_op jit(solution)/shard_map/sweep/pallas_call | solution.py:281
  (10 shorter events, 0.0 us)
Async XLA Ops:
  1.5 8.2 %collective-permute-start = (s32[2,3]{1,0:T(2,128)S(1)}, s32[2,3]{1,0:T(2,128)S(1)}, u32[]{:S(2)}, u32[]{:S(2)}) collective-permute-start(s32[2,3]{1,0:T(2,128)S(1)} %pad_add_fusion.refs_0_), channel_id=1, source_target_pairs={{0,8},{8,16},{16,24},{24,0},{1,9},{9,17},{17,25},{25,1},{2,10},{10... | collective-permute-start | bytes 80 | tf_op jit(solution)/shard_map/ppermute | solution.py:242
  1.9 9.3 %collective-permute-start.1 = (s32[2,3]{1,0:T(2,128)S(1)}, s32[2,3]{1,0:T(2,128)S(1)}, u32[]{:S(2)}, u32[]{:S(2)}) collective-permute-start(s32[2,3]{1,0:T(2,128)S(1)} %pad_add_fusion.refs_0_), channel_id=1, source_target_pairs={{0,16},{8,24},{16,0},{24,8},{1,17},{9,25},{17,1},{25,9},{2,18},{10... | collective-permute-start | bytes 80 | tf_op jit(solution)/shard_map/ppermute | solution.py:242
  4.5 6.8 %collective-permute-start.2 = (s32[2,3]{1,0:T(2,128)S(1)}, s32[2,3]{1,0:T(2,128)S(1)}, u32[]{:S(2)}, u32[]{:S(2)}) collective-permute-start(s32[2,3]{1,0:T(2,128)S(1)} %pad_add_fusion.refs_0_), channel_id=1, source_target_pairs={{0,24},{8,0},{16,8},{24,16},{1,25},{9,1},{17,9},{25,17},{2,26},{10... | collective-permute-start | bytes 80 | tf_op jit(solution)/shard_map/ppermute | solution.py:242
  5.9 20.4 %copy-start = (f32[4,320,320]{2,1,0:T(8,128)S(1)}, f32[4,320,320]{2,1,0:T(8,128)}, u32[]{:S(2)}) copy-start(f32[4,320,320]{2,1,0:T(8,128)} %library.1) | copy-start | bytes 4915204
  5.9 20.4 %copy-start.1 = (f32[1,1,2,64,320]{4,3,2,1,0:T(8,128)S(1)}, f32[1,1,2,64,320]{4,3,2,1,0:T(8,128)}, u32[]{:S(2)}) copy-start(f32[1,1,2,64,320]{4,3,2,1,0:T(8,128)} %param.8) | copy-start | bytes 491524
  5.9 20.4 %copy-start.2 = (s32[1,1,2,4]{3,2,1,0:T(2,128)S(1)}, s32[1,1,2,4]{3,2,1,0:T(2,128)}, u32[]{:S(2)}) copy-start(s32[1,1,2,4]{3,2,1,0:T(2,128)} %param.15) | copy-start | bytes 100
  5.9 20.4 %collective-permute-start.3 = (f32[2,64,320]{2,1,0:T(8,128)}, f32[2,64,320]{2,1,0:T(8,128)S(1)}, u32[]{:S(2)}, u32[]{:S(2)}) collective-permute-start(f32[2,64,320]{2,1,0:T(8,128)} %bitcast.9), channel_id=1, source_target_pairs={{0,2},{2,4},{4,6},{6,0},{1,3},{3,5},{5,7},{7,1},{8,10},{10,12},{12... | collective-permute-start | bytes 491528 | tf_op jit(solution)/shard_map/ppermute | solution.py:242
  7.5 18.8 %collective-permute-start.4 = (f32[2,64,320]{2,1,0:T(8,128)}, f32[2,64,320]{2,1,0:T(8,128)S(1)}, u32[]{:S(2)}, u32[]{:S(2)}) collective-permute-start(f32[2,64,320]{2,1,0:T(8,128)} %bitcast.10), channel_id=1, source_target_pairs={{0,6},{2,0},{4,2},{6,4},{1,7},{3,1},{5,3},{7,5},{8,14},{10,8},{12,... | collective-permute-start | bytes 491528 | tf_op jit(solution)/shard_map/ppermute | solution.py:242
  9.7 16.5 %collective-permute-start.5 = (f32[2,64,320]{2,1,0:T(8,128)}, f32[2,64,320]{2,1,0:T(8,128)S(1)}, u32[]{:S(2)}, u32[]{:S(2)}) collective-permute-start(f32[2,64,320]{2,1,0:T(8,128)} %bitcast.11), channel_id=1, source_target_pairs={{0,1},{1,0},{2,3},{3,2},{4,5},{5,4},{6,7},{7,6},{8,9},{9,8},{10,11... | collective-permute-start | bytes 491528 | tf_op jit(solution)/shard_map/ppermute | solution.py:242
  11.3 1.4 %copy-start.3 = (f32[3,320,320]{2,1,0:T(8,128)S(1)}, f32[3,320,320]{2,1,0:T(8,128)}, u32[]{:S(2)}) copy-start(f32[3,320,320]{2,1,0:T(8,128)} %refs_5_.3) | copy-start | bytes 3686404
  12.6 0.7 copy-start.4
  28.8 16.4 %collective-permute-start.6 = (f32[2,64,320]{2,1,0:T(8,128)S(1)}, f32[2,64,320]{2,1,0:T(8,128)S(1)}, u32[]{:S(2)}, u32[]{:S(2)}) collective-permute-start(f32[2,64,320]{2,1,0:T(8,128)S(1)} %residual.1.refs_0_), channel_id=1, source_target_pairs={{0,8},{8,16},{16,24},{24,0},{1,9},{9,17},{17,25},{25,1},{2,10},{10... | collective-permute-start | bytes 491528 | tf_op jit(solution)/shard_map/ppermute | solution.py:242
  28.9 16.4 %collective-permute-start.7 = (f32[2,64,320]{2,1,0:T(8,128)S(1)}, f32[2,64,320]{2,1,0:T(8,128)S(1)}, u32[]{:S(2)}, u32[]{:S(2)}) collective-permute-start(f32[2,64,320]{2,1,0:T(8,128)S(1)} %residual.1.refs_0_), channel_id=1, source_target_pairs={{0,16},{8,24},{16,0},{24,8},{1,17},{9,25},{17,1},{25,9},{2,18},{10... | collective-permute-start | bytes 491528 | tf_op jit(solution)/shard_map/ppermute | solution.py:242
  29.5 15.8 %collective-permute-start.8 = (f32[2,64,320]{2,1,0:T(8,128)S(1)}, f32[2,64,320]{2,1,0:T(8,128)S(1)}, u32[]{:S(2)}, u32[]{:S(2)}) collective-permute-start(f32[2,64,320]{2,1,0:T(8,128)S(1)} %residual.1.refs_0_), channel_id=1, source_target_pairs={{0,24},{8,0},{16,8},{24,16},{1,25},{9,1},{17,9},{25,17},{2,26},{10... | collective-permute-start | bytes 491528 | tf_op jit(solution)/shard_map/ppermute | solution.py:242

commit v3 on v2

--- a/solution.py
+++ b/solution.py
@@ -9,7 +9,7 @@
 F32 = jnp.float32
 BF16 = jnp.bfloat16
 LOW_STEPS = 2
-HIGH_STEPS = 4
+HIGH_STEPS = 12
 CONVERGED = 0.08
 
 
@@ -24,9 +24,10 @@
 
 
 def dot3(a, b, transposed=False):
-    return (
-        dot(a[0], b[0], transposed) + (dot(a[0], b[1], transposed) + dot(a[1], b[0], transposed))
-    )
+    if transposed:
+        return dot(a[0], b[0], True) + (dot(a[0], b[1], True) + dot(a[1], b[0], True))
+    left = jnp.concatenate([a[0], a[0], a[1]], axis=1)
+    return dot(left, jnp.concatenate([b[0], b[1], b[0]], axis=0))
 
 
 def eye_mask(size):
@@ -64,19 +65,22 @@
     return jnp.sum(jnp.sum(r * r, axis=0, keepdims=True), axis=1, keepdims=True)
 
 
-def invert(a_refs, x_refs):
+def invert(a_refs, x_refs, low_steps=LOW_STEPS):
     size = a_refs[0].shape[0]
     pairs = list(zip(a_refs, x_refs))
     mask = eye_mask(size)
     lows, xs = [], []
     for a_ref, unused in pairs:
         a = a_ref[...]
-        trace = jnp.sum(jnp.sum(jnp.where(mask, a, 0.0), axis=0, keepdims=True), axis=1, keepdims=True)
-        square = jnp.sum(jnp.sum(a * a, axis=0, keepdims=True), axis=1, keepdims=True)
-        scale = trace / square
-        xs.append(jnp.where(mask, 2.0 * scale, 0.0) - (scale * scale) * a)
+        diagonal = jnp.where(mask, a, 0.0)
+        row = 1.0 / jnp.sum(diagonal, axis=0, keepdims=True)
+        col = 1.0 / jnp.sum(diagonal, axis=1, keepdims=True)
+        scaled = a * row * col
+        square = jnp.sum(jnp.sum(a * scaled, axis=0, keepdims=True), axis=1, keepdims=True)
+        scale = size / square
+        xs.append(jnp.where(mask, 2.0 * scale * row, 0.0) - (scale * scale) * scaled)
         lows.append(a.astype(BF16))
-    for step in range(LOW_STEPS):
+    for step in range(low_steps):
         xbs = [x.astype(BF16) for x in xs]
         rs = [jnp.where(mask, 1.0, 0.0) - dot(low, xb) for low, xb in zip(lows, xbs)]
         xs = [x + dot(xb, r.astype(BF16)) for x, xb, r in zip(xs, xbs, rs)]
@@ -86,6 +90,14 @@
 
     @pl.when(jnp.logical_not(worst < CONVERGED**2))
     def _():
+        @pl.when(jnp.logical_not(worst < 0.25))
+        def _():
+            for a_ref, x_ref in pairs:
+                a = a_ref[...]
+                row = 1.0 / jnp.sum(jnp.where(mask, a, 0.0), axis=0, keepdims=True)
+                norm = jnp.max(jnp.sum(jnp.abs(a) * row, axis=1, keepdims=True), axis=0, keepdims=True)
+                x_ref[...] = jnp.where(mask, row / norm, 0.0)
+
         def again(state):
             step, now = state
             return jnp.logical_and(step < HIGH_STEPS, jnp.logical_not(now < CONVERGED**2))
@@ -189,7 +201,7 @@
         slot = 2 * (level - base) + (side if level < half - 1 else 0)
         return store[2 * which][slot], store[2 * which + 1][slot]
 
-    invert([schur.at[0]], [inverse])
+    invert([schur.at[0]], [inverse], 1)
     carried = [None] * count
     low, high = residual[0], residual[count - 1]
     for i in range(half):

time: 109 us -> 45.9 us (0.42)
  Pallas kernels: 92.6 us -> 30.1 us
    pallas_call x1, Pallas kernels: 62.8 us -> 6.63 us  [on_device(): pl.pallas_call(functools.partial(sweep_kernel, wall_count, cut), out_shap...]
    pallas_call x2, Pallas kernels: 27.3 us -> 20.9 us  [factor(): pl.pallas_call(functools.partial(levels_kernel, first, last, wall_count,...]
  transfers between devices with their start and end apart: 9 -> 9, of which waited for: 0 -> 0; matrix products, arithmetic and copies ran while one was open for 0% -> 0% of each run, Pallas kernels for 25% -> 46%
where the time goes in v3:
time: 45.9 us; the launch traced here: 45.6 us
  Pallas kernels  30.1 us (66%)
  starting transfers between devices  11.8 us (26%)
  local copies, waits for them, and re-layouts  2.83 us (6%)
  other arithmetic  0.75 us (2%)
    pallas_call x2, Pallas kernels, factor(): pl.pallas_call(functools.partial(levels_kernel, first, last, wall_count,...  20.9 us
    ppermute x9, starting transfers between devices, shifted(): return lax.ppermute(array, axis, [(i, (i + shift) % n) for i in range(n)])  11.8 us
    pallas_call x1, Pallas kernels, on_device(): pl.pallas_call(functools.partial(sweep_kernel, wall_count, cut), out_shap...  6.63 us
    pallas_call x1, Pallas kernels, on_device(): pl.pallas_call(residual_kernel, out_shape=jax.ShapeDtypeStruct(own.shape,...  2.52 us
    unnamed x10, local copies, waits for them, and re-layouts  2.09 us
  transfers between devices with their start and end apart: 9, of which 0 were waited for; matrix products, arithmetic and copies ran while one was open for 0% of the time, Pallas kernels for 46%

profile of v3, /device:TPU:0, one launch (start us, length us, event | category | flops | bytes accessed | tf_op | source)
XLA Modules:
  0.0 45.6 jit_solution(9492733513846152785)
XLA Ops:
  0.0 0.7 %copy.9 = s32[2,1]{1,0:T(2,128)S(1)} copy(s32[2,1]{0,1:T(1,128)} %bitcast.12) | data formatting | bytes 16 | tf_op jit(solution)/shard_map/broadcast_in_dim;squeeze | solution.py:256
  0.7 0.8 %pad_add_fusion.refs_0_ = s32[2,3]{1,0:T(2,128)S(1)} fusion(s32[2,2]{1,0:T(2,128)} %bitcast.8, s32[2,1]{1,0:T(2,128)S(1)} %copy.9), kind=kLoop, calls=%fused_computation | loop fusion | flops 6 | bytes 48 | tf_op jit(solution)/shard_map/concatenate | solution.py:256
  1.5 0.5 collective-permute-start
  1.9 2.5 %collective-permute-start.1 = (s32[2,3]{1,0:T(2,128)S(1)}, s32[2,3]{1,0:T(2,128)S(1)}, u32[]{:S(2)}, u32[]{:S(2)}) collective-permute-start(s32[2,3]{1,0:T(2,128)S(1)} %pad_add_fusion.refs_0_), channel_id=1, source_target_pairs={{0,16},{8,24},{16,0},{24,8},{1,17},{9,25},{17,1},{25,9},{2,18},{10... | collective-permute-start | bytes 80 | tf_op jit(solution)/shard_map/ppermute | solution.py:254
  4.5 1.4 %collective-permute-start.2 = (s32[2,3]{1,0:T(2,128)S(1)}, s32[2,3]{1,0:T(2,128)S(1)}, u32[]{:S(2)}, u32[]{:S(2)}) collective-permute-start(s32[2,3]{1,0:T(2,128)S(1)} %pad_add_fusion.refs_0_), channel_id=1, source_target_pairs={{0,24},{8,0},{16,8},{24,16},{1,25},{9,1},{17,9},{25,17},{2,26},{10... | collective-permute-start | bytes 80 | tf_op jit(solution)/shard_map/ppermute | solution.py:254
  5.9 1.6 %collective-permute-start.3 = (f32[2,64,320]{2,1,0:T(8,128)}, f32[2,64,320]{2,1,0:T(8,128)S(1)}, u32[]{:S(2)}, u32[]{:S(2)}) collective-permute-start(f32[2,64,320]{2,1,0:T(8,128)} %bitcast.9), channel_id=1, source_target_pairs={{0,2},{2,4},{4,6},{6,0},{1,3},{3,5},{5,7},{7,1},{8,10},{10,12},{12... | collective-permute-start | bytes 491528 | tf_op jit(solution)/shard_map/ppermute | solution.py:254
  7.5 2.2 %collective-permute-start.4 = (f32[2,64,320]{2,1,0:T(8,128)}, f32[2,64,320]{2,1,0:T(8,128)S(1)}, u32[]{:S(2)}, u32[]{:S(2)}) collective-permute-start(f32[2,64,320]{2,1,0:T(8,128)} %bitcast.10), channel_id=1, source_target_pairs={{0,6},{2,0},{4,2},{6,4},{1,7},{3,1},{5,3},{7,5},{8,14},{10,8},{12,... | collective-permute-start | bytes 491528 | tf_op jit(solution)/shard_map/ppermute | solution.py:254
  9.7 0.0 collective-permute-done.refs_1_
  9.7 1.5 %collective-permute-start.5 = (f32[2,64,320]{2,1,0:T(8,128)}, f32[2,64,320]{2,1,0:T(8,128)S(1)}, u32[]{:S(2)}, u32[]{:S(2)}) collective-permute-start(f32[2,64,320]{2,1,0:T(8,128)} %bitcast.11), channel_id=1, source_target_pairs={{0,1},{1,0},{2,3},{3,2},{4,5},{5,4},{6,7},{7,6},{8,9},{9,8},{10,11... | collective-permute-start | bytes 491528 | tf_op jit(solution)/shard_map/ppermute | solution.py:254
  11.3 0.0 collective-permute-done.1.refs_2_
  11.3 0.0 collective-permute-done.2.refs_3_
  11.3 1.4 %copy-done.3 = f32[3,320,320]{2,1,0:T(8,128)S(1)} copy-done((f32[3,320,320]{2,1,0:T(8,128)S(1)}, f32[3,320,320]{2,1,0:T(8,128)}, u32[]{:S(2)}) %copy-start.3) | copy-done | bytes 1228824
  12.6 0.7 %copy-done.4 = f32[8,320]{1,0:T(8,128)S(1)} copy-done((f32[8,320]{1,0:T(8,128)S(1)}, f32[8,320]{1,0:T(8,128)}, u32[]{:S(2)}) %copy-start.4) | copy-done | bytes 10264
  13.3 11.4 %factor_outer.1 = (f32[2,320,320]{2,1,0:T(8,128)S(1)}, bf16[4,320,320]{2,1,0:T(8,128)(2,1)S(1)}, bf16[4,320,320]{2,1,0:T(8,128)(2,1)S(1)}, bf16[4,320,320]{2,1,0:T(8,128)(2,1)S(1)}, bf16[4,320,320]{2,1,0:T(8,128)(2,1)S(1)}) custom-call(s32[2,3]{1,0:T(2,128)S(1)} %pad_add_fusion.refs_0_, s32[2,3]{1,0:T(2,128)S(1)} %collective-permute-done.refs_1_, ...), custom_call_target="tpu_custom_call" | custom-call | flops 20971520000 | bytes 1638400 | tf_op jit(solution)/shard_map/factor_outer/pallas_call | solution.py:266
  24.7 0.0 collective-permute-done.4.near_1
  24.7 0.0 collective-permute-done.5.near_2.near_3
  24.8 2.5 %residual.1.refs_0_ = f32[2,64,320]{2,1,0:T(8,128)S(1)} custom-call(s32[2,4]{1,0:T(2,128)S(1)} %bitcast.7, f32[2,64,320]{2,1,0:T(8,128)S(1)} %bitcast.6, f32[2,64,320]{2,1,0:T(8,128)S(1)} %collective-permute-done.3.near_0, f32[2,64,320]{2,1,0:T(8,128)S(1)} %collective-permute-done.4.near_1, f32[2,64,320]{2,1,0:T(8,128)S(1)} %collective-permute-done.5.near_2.near_3, ...), custom_call_target="tpu_custom_call" | custom-call | tf_op jit(solution)/shard_map/residual/pallas_call | solution.py:282
  27.3 0.1 collective-permute-start.6
  27.4 0.6 %collective-permute-start.7 = (f32[2,64,320]{2,1,0:T(8,128)S(1)}, f32[2,64,320]{2,1,0:T(8,128)S(1)}, u32[]{:S(2)}, u32[]{:S(2)}) collective-permute-start(f32[2,64,320]{2,1,0:T(8,128)S(1)} %residual.1.refs_0_), channel_id=1, source_target_pairs={{0,16},{8,24},{16,0},{24,8},{1,17},{9,25},{17,1},{25,9},{2,18},{10... | collective-permute-start | bytes 491528 | tf_op jit(solution)/shard_map/ppermute | solution.py:254
  28.0 1.4 %collective-permute-start.8 = (f32[2,64,320]{2,1,0:T(8,128)S(1)}, f32[2,64,320]{2,1,0:T(8,128)S(1)}, u32[]{:S(2)}, u32[]{:S(2)}) collective-permute-start(f32[2,64,320]{2,1,0:T(8,128)S(1)} %residual.1.refs_0_), channel_id=1, source_target_pairs={{0,24},{8,0},{16,8},{24,16},{1,25},{9,1},{17,9},{25,17},{2,26},{10... | collective-permute-start | bytes 491528 | tf_op jit(solution)/shard_map/ppermute | solution.py:254
  29.4 9.6 %factor_inner.1 = (f32[2,320,320]{2,1,0:T(8,128)S(1)}, bf16[3,320,320]{2,1,0:T(8,128)(2,1)S(1)}, bf16[3,320,320]{2,1,0:T(8,128)(2,1)S(1)}, bf16[3,320,320]{2,1,0:T(8,128)(2,1)S(1)}, bf16[3,320,320]{2,1,0:T(8,128)(2,1)S(1)}) custom-call(s32[2,3]{1,0:T(2,128)S(1)} %pad_add_fusion.refs_0_, s32[2,3]{1,0:T(2,128)S(1)} %collective-permute-done.refs_1_, ...), custom_call_target="tpu_custom_call" | custom-call | flops 15728640000 | bytes 1638400 | tf_op jit(solution)/shard_map/factor_inner/pallas_call | solution.py:266
  39.0 0.0 collective-permute-done.6.refs_1_
  39.0 0.0 collective-permute-done.7.refs_2_
  39.0 6.6 %sweep.1 = f32[2,64,320]{2,1,0:T(8,128)} custom-call(f32[2,64,320]{2,1,0:T(8,128)S(1)} %residual.1.refs_0_, f32[2,64,320]{2,1,0:T(8,128)S(1)} %collective-permute-done.6.refs_1_, f32[2,64,320]{2,1,0:T(8,128)S(1)} %collective-permute-done.7.refs_2_, f32[2,64,320]{2,1,0:T(8,128)S(1)} %collective-permute-done.8.refs_3_, ...), custom_call_target="tpu_custom_call" | custom-call | tf_op jit(solution)/shard_map/sweep/pallas_call | solution.py:293
  (10 shorter events, 0.0 us)
Async XLA Ops:
  1.5 8.2 %collective-permute-start = (s32[2,3]{1,0:T(2,128)S(1)}, s32[2,3]{1,0:T(2,128)S(1)}, u32[]{:S(2)}, u32[]{:S(2)}) collective-permute-start(s32[2,3]{1,0:T(2,128)S(1)} %pad_add_fusion.refs_0_), channel_id=1, source_target_pairs={{0,8},{8,16},{16,24},{24,0},{1,9},{9,17},{17,25},{25,1},{2,10},{10... | collective-permute-start | bytes 80 | tf_op jit(solution)/shard_map/ppermute | solution.py:254
  1.9 9.3 %collective-permute-start.1 = (s32[2,3]{1,0:T(2,128)S(1)}, s32[2,3]{1,0:T(2,128)S(1)}, u32[]{:S(2)}, u32[]{:S(2)}) collective-permute-start(s32[2,3]{1,0:T(2,128)S(1)} %pad_add_fusion.refs_0_), channel_id=1, source_target_pairs={{0,16},{8,24},{16,0},{24,8},{1,17},{9,25},{17,1},{25,9},{2,18},{10... | collective-permute-start | bytes 80 | tf_op jit(solution)/shard_map/ppermute | solution.py:254
  4.5 6.8 %collective-permute-start.2 = (s32[2,3]{1,0:T(2,128)S(1)}, s32[2,3]{1,0:T(2,128)S(1)}, u32[]{:S(2)}, u32[]{:S(2)}) collective-permute-start(s32[2,3]{1,0:T(2,128)S(1)} %pad_add_fusion.refs_0_), channel_id=1, source_target_pairs={{0,24},{8,0},{16,8},{24,16},{1,25},{9,1},{17,9},{25,17},{2,26},{10... | collective-permute-start | bytes 80 | tf_op jit(solution)/shard_map/ppermute | solution.py:254
  5.9 18.9 %copy-start = (f32[4,320,320]{2,1,0:T(8,128)S(1)}, f32[4,320,320]{2,1,0:T(8,128)}, u32[]{:S(2)}) copy-start(f32[4,320,320]{2,1,0:T(8,128)} %library.1) | copy-start | bytes 4915204
  5.9 18.9 %copy-start.1 = (f32[1,1,2,64,320]{4,3,2,1,0:T(8,128)S(1)}, f32[1,1,2,64,320]{4,3,2,1,0:T(8,128)}, u32[]{:S(2)}) copy-start(f32[1,1,2,64,320]{4,3,2,1,0:T(8,128)} %param.8) | copy-start | bytes 491524
  5.9 18.9 %copy-start.2 = (s32[1,1,2,4]{3,2,1,0:T(2,128)S(1)}, s32[1,1,2,4]{3,2,1,0:T(2,128)}, u32[]{:S(2)}) copy-start(s32[1,1,2,4]{3,2,1,0:T(2,128)} %param.15) | copy-start | bytes 100
  5.9 18.8 %collective-permute-start.3 = (f32[2,64,320]{2,1,0:T(8,128)}, f32[2,64,320]{2,1,0:T(8,128)S(1)}, u32[]{:S(2)}, u32[]{:S(2)}) collective-permute-start(f32[2,64,320]{2,1,0:T(8,128)} %bitcast.9), channel_id=1, source_target_pairs={{0,2},{2,4},{4,6},{6,0},{1,3},{3,5},{5,7},{7,1},{8,10},{10,12},{12... | collective-permute-start | bytes 491528 | tf_op jit(solution)/shard_map/ppermute | solution.py:254
  7.5 17.2 %collective-permute-start.4 = (f32[2,64,320]{2,1,0:T(8,128)}, f32[2,64,320]{2,1,0:T(8,128)S(1)}, u32[]{:S(2)}, u32[]{:S(2)}) collective-permute-start(f32[2,64,320]{2,1,0:T(8,128)} %bitcast.10), channel_id=1, source_target_pairs={{0,6},{2,0},{4,2},{6,4},{1,7},{3,1},{5,3},{7,5},{8,14},{10,8},{12,... | collective-permute-start | bytes 491528 | tf_op jit(solution)/shard_map/ppermute | solution.py:254
  9.7 15.0 %collective-permute-start.5 = (f32[2,64,320]{2,1,0:T(8,128)}, f32[2,64,320]{2,1,0:T(8,128)S(1)}, u32[]{:S(2)}, u32[]{:S(2)}) collective-permute-start(f32[2,64,320]{2,1,0:T(8,128)} %bitcast.11), channel_id=1, source_target_pairs={{0,1},{1,0},{2,3},{3,2},{4,5},{5,4},{6,7},{7,6},{8,9},{9,8},{10,11... | collective-permute-start | bytes 491528 | tf_op jit(solution)/shard_map/ppermute | solution.py:254
  11.3 1.4 %copy-start.3 = (f32[3,320,320]{2,1,0:T(8,128)S(1)}, f32[3,320,320]{2,1,0:T(8,128)}, u32[]{:S(2)}) copy-start(f32[3,320,320]{2,1,0:T(8,128)} %refs_5_.3) | copy-start | bytes 3686404
  12.6 0.7 %copy-start.4 = (f32[8,320]{1,0:T(8,128)S(1)}, f32[8,320]{1,0:T(8,128)}, u32[]{:S(2)}) copy-start(f32[8,320]{1,0:T(8,128)} %refs_4_.3) | copy-start | bytes 30724
  27.3 11.7 %collective-permute-start.6 = (f32[2,64,320]{2,1,0:T(8,128)S(1)}, f32[2,64,320]{2,1,0:T(8,128)S(1)}, u32[]{:S(2)}, u32[]{:S(2)}) collective-permute-start(f32[2,64,320]{2,1,0:T(8,128)S(1)} %residual.1.refs_0_), channel_id=1, source_target_pairs={{0,8},{8,16},{16,24},{24,0},{1,9},{9,17},{17,25},{25,1},{2,10},{10... | collective-permute-start | bytes 491528 | tf_op jit(solution)/shard_map/ppermute | solution.py:254
  27.4 11.6 %collective-permute-start.7 = (f32[2,64,320]{2,1,0:T(8,128)S(1)}, f32[2,64,320]{2,1,0:T(8,128)S(1)}, u32[]{:S(2)}, u32[]{:S(2)}) collective-permute-start(f32[2,64,320]{2,1,0:T(8,128)S(1)} %residual.1.refs_0_), channel_id=1, source_target_pairs={{0,16},{8,24},{16,0},{24,8},{1,17},{9,25},{17,1},{25,9},{2,18},{10... | collective-permute-start | bytes 491528 | tf_op jit(solution)/shard_map/ppermute | solution.py:254
  28.0 11.0 %collective-permute-start.8 = (f32[2,64,320]{2,1,0:T(8,128)S(1)}, f32[2,64,320]{2,1,0:T(8,128)S(1)}, u32[]{:S(2)}, u32[]{:S(2)}) collective-permute-start(f32[2,64,320]{2,1,0:T(8,128)S(1)} %residual.1.refs_0_), channel_id=1, source_target_pairs={{0,24},{8,0},{16,8},{24,16},{1,25},{9,1},{17,9},{25,17},{2,26},{10... | collective-permute-start | bytes 491528 | tf_op jit(solution)/shard_map/ppermute | solution.py:254

commit v4 on v1

v4 whole, which is shorter than its diff:
```python
import functools
import jax
import jax.numpy as jnp
from jax import lax
from jax.experimental import pallas as pl
from jax.experimental.pallas import tpu as pltpu
from jax.sharding import PartitionSpec as P

F32 = jnp.float32
BF16 = jnp.bfloat16
LOW_STEPS = 2
CONVERGED = 0.08
MESH = pl.DeviceIdType.MESH


def dot(a, b, transposed=False):
    dims = (((1,), (1,)), ((), ())) if transposed else (((1,), (0,)), ((), ()))
    return lax.dot_general(a, b, dims, preferred_element_type=F32)


def split(a):
    high = a.astype(BF16)
    return high, (a - high.astype(F32)).astype(BF16)


def dot3(a, b, transposed=False):
    if transposed:
        return dot(a[0], b[0], True) + (dot(a[0], b[1], True) + dot(a[1], b[0], True))
    left = jnp.concatenate([a[0], a[0], a[1]], axis=1)
    return dot(left, jnp.concatenate([b[0], b[1], b[0]], axis=0))


def eye_mask(size):
    row = lax.broadcasted_iota(jnp.int32, (size, size), 0)
    col = lax.broadcasted_iota(jnp.int32, (size, size), 1)
    return row == col


def gauss_jordan(a_ref, x_ref):
    size = a_ref.shape[0]
    x_ref[...] = a_ref[...]

    def step(k, unused):
        current = x_ref[...]
        lanes = lax.broadcasted_iota(jnp.int32, (1, size), 1)
        rows = lax.broadcasted_iota(jnp.int32, (size, 1), 0)
        row = x_ref[pl.ds(k, 1), :]
        pivot = jnp.sum(jnp.where(lanes == k, row, 0.0), axis=1, keepdims=True)
        column = jnp.sum(jnp.where(lanes == k, current, 0.0), axis=1, keepdims=True)
        column = jnp.where(rows == k, 0.0, column)
        scaled = jnp.where(lanes == k, 1.0, row) / pivot
        updated = jnp.where(lanes == k, 0.0, current) - column * scaled
        x_ref[...] = jnp.where(rows == k, scaled, updated)
        return unused

    lax.fori_loop(0, size, step, 0)


def invert(blocks, low_steps=LOW_STEPS):
    size = blocks[0].shape[0]
    mask = eye_mask(size)
    xs = []
    for a in blocks:
        diagonal = jnp.where(mask, a, 0.0)
        row = 1.0 / jnp.sum(diagonal, axis=0, keepdims=True)
        col = 1.0 / jnp.sum(diagonal, axis=1, keepdims=True)
        scaled = a * row * col
        square = jnp.sum(jnp.sum(a * scaled, axis=0, keepdims=True), axis=1, keepdims=True)
        scale = size / square
        xs.append(jnp.where(mask, 2.0 * scale * row, 0.0) - (scale * scale) * scaled)
    parts = [split(a) for a in blocks]
    for step in range(low_steps):
        xbs = [x.astype(BF16) for x in xs]
        rs = [jnp.where(mask, 1.0, 0.0) - dot(a[0], xb) for a, xb in zip(parts, xbs)]
        xs = [x + dot(xb, r.astype(BF16)) for x, xb, r in zip(xs, xbs, rs)]
    halves = [split(x) for x in xs]
    rs = [jnp.where(mask, 1.0, 0.0) - dot3(a, x) for a, x in zip(parts, halves)]
    rbs = [r.astype(BF16) for r in rs]
    ts = [r + dot(rb, rb) for r, rb in zip(rs, rbs)]
    xs = [x + dot(h[0], t.astype(BF16)) for x, h, t in zip(xs, halves, ts)]
    missed = jnp.zeros((1, 1), F32)
    for r in rs:
        square = jnp.sum(jnp.sum(r * r, axis=0, keepdims=True), axis=1, keepdims=True)
        missed = missed + jnp.where(square < CONVERGED**2, 0.0, 1.0)
    return xs, missed


class Line:
    def __init__(self, index, mine, library, walls):
        self.library, self.walls = library, walls
        self.rates, self.faces = [], []
        for owner in range(index.shape[0]):
            rows = index[owner]
            for e in range(mine):
                self.rates.append(rows[e, 0])
                self.faces.append(rows[e, 1])
        self.faces.append(rows[mine - 1, 2])
        self.count = len(self.rates)
        self.size = walls.shape[1]

    def face(self, i):
        return self.walls[self.faces[i]]

    def block(self, i):
        row = self.library[pl.ds(self.rates[i], 1), :]
        return jnp.where(eye_mask(self.size), row, 0.0) + self.face(i) + self.face(i + 1)


def keep(i, x, coupling, stores):
    xs = split(x)
    q = split(coupling)
    gs = split(dot3(xs, q))
    for store, value in zip(stores, xs + gs):
        store[i] = value
    return dot3(q, gs)


class Sweep:
    def __init__(self, count, stores, residual):
        self.count, self.half, self.stores, self.residual = count, count // 2, stores, residual

    def pivot(self, i):
        return self.stores[0][i], self.stores[1][i]

    def step(self, i):
        return self.stores[2][i], self.stores[3][i]

    def forward(self):
        count, half, residual = self.count, self.half, self.residual
        carried = [None] * count
        low, high = residual(0), residual(count - 1)
        for i in range(half):
            j = count - 1 - i
            carried[i], carried[j] = split(low), split(high)
            if i + 1 < half:
                low = residual(i + 1) + dot3(carried[i], self.step(i))
                high = residual(j - 1) + dot3(carried[j], self.step(j))
        skip = (half - 1, half)
        self.scaled = {
            i: dot3(carried[i], self.pivot(i)) for i in range(count) if i not in skip
        }
        self.low, self.carried = low, carried[half]

    def back(self, inverse, values):
        count, half = self.count, self.half
        low = self.low + dot3(self.carried, self.step(half))
        middle = dot3(self.carried, self.pivot(half))
        low = dot3(split(low), split(inverse))
        values[half - 1] = low
        lows = split(low)
        high = middle + dot3(lows, self.step(half), True)
        values[half] = high
        highs = split(high)
        for i in range(half - 2, -1, -1):
            j = count - 1 - i
            low = self.scaled[i] + dot3(lows, self.step(i), True)
            high = self.scaled[j] + dot3(highs, self.step(j), True)
            values[i] = low
            values[j] = high
            lows, highs = split(low), split(high)


def line_kernel(
    rates, faces, neighbours, side_in, old, library_in, walls_in, blocks_in,
    out, sides_out, index_out, missed_out,
    side, library, walls, blocks, index, halo, sides, values, ph, plo, gh, glo,
    local_sem, index_send, index_recv, halo_send, halo_recv, side_send, side_recv,
):
    n = lax.axis_size("wall")
    place = lax.axis_index("wall")
    mine = side.shape[0]
    count = n * mine
    half = count // 2
    top = count - 1

    pairs = ((walls_in, walls), (library_in, library), (side_in.at[0, 0], side), (blocks_in, blocks))
    loads = [
        pltpu.make_async_copy(src, dst, local_sem.at[k]) for k, (src, dst) in enumerate(pairs)
    ]
    for load in loads:
        load.start()

    row = lax.broadcasted_iota(jnp.int32, index.shape[1:], 0)
    col = lax.broadcasted_iota(jnp.int32, index.shape[1:], 1)
    own = jnp.zeros(index.shape[1:], jnp.int32)
    for e in range(mine):
        for c, value in enumerate((rates[0, 0, e], faces[0, 0, e, 0], faces[0, 0, e, 1])):
            own = jnp.where(jnp.logical_and(row == e, col == c), value, own)
    index[place] = own

    partners = [{"wall": lax.rem(place + s, n)} for s in range(1, n)]
    beside = []
    for base, axis in ((0, "span"), (2, "stream")):
        m = lax.axis_size(axis)
        here = lax.axis_index(axis)
        beside.append((base, {axis: lax.rem(here + 1, m)}))
        if m > 2:
            beside.append((base + 1, {axis: lax.rem(here + m - 1, m)}))
    barrier = pltpu.get_barrier_semaphore()
    for target in partners + [target for unused, target in beside]:
        pl.semaphore_signal(barrier, inc=1, device_id=target, device_id_type=MESH)
    pl.semaphore_wait(barrier, len(partners) + len(beside))

    def spread(buffer, send, recv):
        copies = [
            pltpu.make_async_remote_copy(
                src_ref=buffer.at[place],
                dst_ref=buffer.at[place],
                send_sem=send.at[k],
                recv_sem=recv.at[k],
                device_id=target,
                device_id_type=MESH,
            )
            for k, target in enumerate(partners)
        ]
        for copy in copies:
            copy.start()
        return copies

    index_copies = spread(index, index_send, index_recv)
    halo_copies = [
        pltpu.make_async_remote_copy(
            src_ref=old.at[0, 0],
            dst_ref=halo.at[k],
            send_sem=halo_send.at[k],
            recv_sem=halo_recv.at[k],
            device_id=target,
            device_id_type=MESH,
        )
        for k, target in beside
    ]
    for copy in halo_copies:
        copy.start()
    for load in loads[:2]:
        load.wait()
    for copy in index_copies:
        copy.wait()
    line = Line(index, mine, library, walls)
    stores = (ph, plo, gh, glo)
    low, high = line.block(0), line.block(top)
    missed = jnp.zeros((1, 1), F32)
    side_copies = None
    for i in range(half - 1):
        j = top - i
        (x, y), off = invert([low, high])
        missed = missed + off
        low = line.block(i + 1) - keep(i, x, line.face(i + 1), stores)
        high = line.block(j - 1) - keep(j, y, line.face(j), stores)
        if i == max(0, half - 3):
            for load in loads[2:]:
                load.wait()
            for copy in halo_copies:
                copy.wait()
            arrived = [k for k, unused in beside]
            for e in range(mine):
                total = side[e]
                for d in range(4):
                    near = halo[d if d in arrived else d - 1, e]
                    block = blocks[neighbours[0, 0, e, d]]
                    total = total - dot3(split(near), split(block), True)
                sides[place, e] = total
            side_copies = spread(sides, side_send, side_recv)
    for copy in side_copies:
        copy.wait()
    sweep = Sweep(count, stores, lambda i: sides[i // mine, i % mine])
    sweep.forward()
    (y,), off = invert([high])
    missed = missed + off
    low = low - keep(half, y, line.face(half), stores)
    (x,), off = invert([low], 1)
    missed = missed + off
    sweep.back(x, values)
    for e in range(mine):
        out[0, 0, e] = values[place * mine + e]
    sides_out[...] = sides[...]
    index_out[...] = index[...]
    missed_out[...] = jnp.broadcast_to(missed, missed_out.shape)


def check_kernel(
    missed, fast, sides_in, index_in, library_in, walls_in,
    out, sides, index, library, walls, values, block, inverse, ph, plo, gh, glo,
):
    out[...] = fast[...]

    @pl.when(jnp.logical_not(missed[0:1, 0:1][0, 0] < 0.5))
    def _():
        for src, dst in (
            (sides_in, sides), (index_in, index), (library_in, library), (walls_in, walls)
        ):
            pltpu.sync_copy(src, dst)
        n, mine = sides.shape[:2]
        count = n * mine
        half = count // 2
        place = lax.axis_index("wall")
        line = Line(index, mine, library, walls)
        stores = (ph, plo, gh, glo)

        def exact(a):
            block[...] = a
            gauss_jordan(block, inverse)
            return inverse[...]

        low = line.block(0)
        high = line.block(count - 1)
        for i in range(half - 1):
            j = count - 1 - i
            low = line.block(i + 1) - keep(i, exact(low), line.face(i + 1), stores)
            high = line.block(j - 1) - keep(j, exact(high), line.face(j), stores)
        sweep = Sweep(count, stores, lambda i: sides[i // mine, i % mine])
        sweep.forward()
        low = low - keep(half, exact(high), line.face(half), stores)
        sweep.back(exact(low), values)
        for e in range(mine):
            out[0, 0, e] = values[place * mine + e]


def on_device(
    right_side,
    old_values,
    element_library,
    wall_library,
    face_library,
    element_index,
    wall_faces,
    face_index,
):
    size = wall_library.shape[1]
    vmem = pl.BlockSpec(memory_space=pltpu.VMEM)
    smem = pl.BlockSpec(memory_space=pltpu.SMEM)
    free = pl.BlockSpec(memory_space=pl.ANY)
    n = lax.axis_size("wall")
    mine = right_side.shape[2]
    count = n * mine
    tail = right_side.shape[3:]
    one = jax.ShapeDtypeStruct(right_side.shape, F32)
    all_sides = jax.ShapeDtypeStruct((n, mine) + tail, F32)
    all_rows = jax.ShapeDtypeStruct((n, 8, 128), jnp.int32)
    stores = [pltpu.VMEM((count, size, size), BF16)] * 4
    fast, sides, index, missed = pl.pallas_call(
        line_kernel,
        out_shape=[one, all_sides, all_rows, jax.ShapeDtypeStruct((8, 128), F32)],
        in_specs=[smem] * 3 + [free] * 5,
        out_specs=[vmem] * 4,
        scratch_shapes=[
            pltpu.VMEM((mine,) + tail, F32),
            pltpu.VMEM(element_library.shape, F32),
            pltpu.VMEM(wall_library.shape, F32),
            pltpu.VMEM(face_library.shape, F32),
            pltpu.VMEM(all_rows.shape, jnp.int32),
            pltpu.VMEM((4, mine) + tail, F32),
            pltpu.VMEM(all_sides.shape, F32),
            pltpu.VMEM((count,) + tail, F32),
            *stores,
            pltpu.SemaphoreType.DMA((4,)),
            pltpu.SemaphoreType.DMA((n - 1,)),
            pltpu.SemaphoreType.DMA((n - 1,)),
            pltpu.SemaphoreType.DMA((4,)),
            pltpu.SemaphoreType.DMA((4,)),
            pltpu.SemaphoreType.DMA((n - 1,)),
            pltpu.SemaphoreType.DMA((n - 1,)),
        ],
        compiler_params=pltpu.CompilerParams(
            vmem_limit_bytes=60 * 1024 * 1024, collective_id=0, has_side_effects=True
        ),
        name="line",
    )(
        element_index, wall_faces, face_index, right_side, old_values,
        element_library, wall_library, face_library,
    )
    return pl.pallas_call(
        check_kernel,
        out_shape=one,
        in_specs=[vmem] * 2 + [free] * 4,
        out_specs=vmem,
        scratch_shapes=[
            pltpu.VMEM(all_sides.shape, F32),
            pltpu.VMEM(all_rows.shape, jnp.int32),
            pltpu.VMEM(element_library.shape, F32),
            pltpu.VMEM(wall_library.shape, F32),
            pltpu.VMEM((count,) + tail, F32),
            pltpu.VMEM((size, size), F32),
            pltpu.VMEM((size, size), F32),
            *stores,
        ],
        compiler_params=pltpu.CompilerParams(vmem_limit_bytes=60 * 1024 * 1024),
        name="check",
    )(missed, fast, sides, index, element_library, wall_library)


def solution(mesh):
    placed = (
        P("span", "stream", "wall", None, None),
        P("span", "stream", "wall", None, None),
        P(),
        P(),
        P(),
        P("span", "stream", "wall"),
        P("span", "stream", "wall", None),
        P("span", "stream", "wall", None),
    )
    return jax.shard_map(
        on_device,
        mesh=mesh,
        in_specs=placed,
        out_specs=P("span", "stream", "wall", None, None),
        check_vma=False,
    )
```

time: 81.5 us -> 462 us (5.67)
  Pallas kernels: 53 us -> 462 us
  blocking collectives: 13.9 us -> 0 us
  starting transfers between devices: 6.57 us -> 0 us
  local copies, waits for them, and re-layouts: 6.16 us -> 0 us
    pallas_call x3 -> x2, Pallas kernels: 53 us -> 462 us  [the longest x1 420 us: on_device(): pl.pallas_call(check_kernel, out_shape=one, in_specs=[vmem] * 2 + [free]...]
    all_gather x2 -> x0, blocking collectives: 13.9 us -> none  [the longest x1 8.87 us: on_device(): residual = lax.all_gather(residual, 'wall', axis=0, tiled=True)]
    ppermute x3 -> x0, starting transfers between devices: 6.57 us -> none  [the longest x1 3.6 us: on_device(): lax.ppermute(own, axis, [((i + 1) % n, i) for i in range(n)])]
    unnamed x18 -> x0, local copies, waits for them, and re-layouts: 4.67 us -> none
  transfers between devices with their start and end apart: 3 -> 0, of which waited for: 0 -> 0; matrix products, arithmetic and copies ran while one was open for 4% -> 0% of each run, Pallas kernels for 53% -> 0%
where the time goes in v4:
time: 462 us
  Pallas kernels  462 us (100%)
    pallas_call x1, Pallas kernels, on_device(): pl.pallas_call(check_kernel, out_shape=one, in_specs=[vmem] * 2 + [free]...  420 us
    pallas_call x1, Pallas kernels, on_device(): pl.pallas_call(line_kernel, out_shape=[one, all_sides, all_rows, jax.Shap...  41.7 us

profile of v4, /device:TPU:0, one launch (start us, length us, event | category | flops | bytes accessed | tf_op | source)
XLA Modules:
  0.0 461.6 jit_solution(3135341634140491567)
XLA Ops:
  0.0 41.7 %line.1 = (f32[1,1,2,64,320]{4,3,2,1,0:T(8,128)}, f32[4,2,64,320]{3,2,1,0:T(8,128)}, s32[4,8,128]{2,1,0:T(8,128)}, f32[8,128]{1,0:T(8,128)}) custom-call(s32[1,1,2]{2,1,0:T(1,128)} %rates.1, s32[1,1,2,2]{3,2,1,0:T(2,128)} %faces.1, s32[1,1,2,4]{3,2,1,0:T(2,128)} %neighbours.1, f32[1,1,2,64,320]{4,3,2,1,0:T(8,128)} %side_in.1, f32[1,1,2,64,320]{4,3,2,1,0:T(8,128)} %old.1, ...), custom_call_target="tpu_custom_call" | custom-call | tf_op jit(solution)/shard_map/line/pallas_call | solution.py:340
  41.7 419.9 %check.1 = f32[1,1,2,64,320]{4,3,2,1,0:T(8,128)} custom-call(f32[8,128]{1,0:T(8,128)} %get-tuple-element.9.missed, f32[1,1,2,64,320]{4,3,2,1,0:T(8,128)} %get-tuple-element.10.fast, f32[4,2,64,320]{3,2,1,0:T(8,128)} %get-tuple-element.11.sides_in, s32[4,8,128]{2,1,0:T(8,128)} %get-tuple-element.12.index_in, f32[8,320]{1,0:T(8,128)} %library_in.3, ...), custom_call_target="tpu_custom_call" | custom-call | tf_op jit(solution)/shard_map/check/pallas_call | solution.py:371

commit v5 on v4

--- a/solution.py
+++ b/solution.py
@@ -9,7 +9,7 @@
 F32 = jnp.float32
 BF16 = jnp.bfloat16
 LOW_STEPS = 2
-CONVERGED = 0.08
+CONVERGED = 6e-4
 MESH = pl.DeviceIdType.MESH
 
 
@@ -65,9 +65,7 @@
         row = 1.0 / jnp.sum(diagonal, axis=0, keepdims=True)
         col = 1.0 / jnp.sum(diagonal, axis=1, keepdims=True)
         scaled = a * row * col
-        square = jnp.sum(jnp.sum(a * scaled, axis=0, keepdims=True), axis=1, keepdims=True)
-        scale = size / square
-        xs.append(jnp.where(mask, 2.0 * scale * row, 0.0) - (scale * scale) * scaled)
+        xs.append(jnp.where(mask, 2.0 * row, 0.0) - scaled)
     parts = [split(a) for a in blocks]
     for step in range(low_steps):
         xbs = [x.astype(BF16) for x in xs]
@@ -76,18 +74,18 @@
     halves = [split(x) for x in xs]
     rs = [jnp.where(mask, 1.0, 0.0) - dot3(a, x) for a, x in zip(parts, halves)]
     rbs = [r.astype(BF16) for r in rs]
-    ts = [r + dot(rb, rb) for r, rb in zip(rs, rbs)]
-    xs = [x + dot(h[0], t.astype(BF16)) for x, h, t in zip(xs, halves, ts)]
+    xs = [x + dot(h[0], rb) for x, h, rb in zip(xs, halves, rbs)]
     missed = jnp.zeros((1, 1), F32)
-    for r in rs:
-        square = jnp.sum(jnp.sum(r * r, axis=0, keepdims=True), axis=1, keepdims=True)
+    for rb in rbs:
+        left = dot(rb, rb)
+        square = jnp.sum(jnp.sum(left * left, axis=0, keepdims=True), axis=1, keepdims=True)
         missed = missed + jnp.where(square < CONVERGED**2, 0.0, 1.0)
     return xs, missed
 
 
 class Line:
-    def __init__(self, index, mine, library, walls):
-        self.library, self.walls = library, walls
+    def __init__(self, index, mine, library, walls, wide, tall):
+        self.library, self.walls, self.wide, self.tall = library, walls, wide, tall
         self.rates, self.faces = [], []
         for owner in range(index.shape[0]):
             rows = index[owner]
@@ -101,18 +99,28 @@
     def face(self, i):
         return self.walls[self.faces[i]]
 
+    def coupling(self, i):
+        return self.wide[self.faces[i]], self.tall[self.faces[i]]
+
     def block(self, i):
         row = self.library[pl.ds(self.rates[i], 1), :]
         return jnp.where(eye_mask(self.size), row, 0.0) + self.face(i) + self.face(i + 1)
 
 
 def keep(i, x, coupling, stores):
+    wide, tall = coupling
     xs = split(x)
-    q = split(coupling)
-    gs = split(dot3(xs, q))
+    gs = split(dot(jnp.concatenate([xs[0], xs[0], xs[1]], axis=1), tall))
     for store, value in zip(stores, xs + gs):
         store[i] = value
-    return dot3(q, gs)
+    return dot(wide, jnp.concatenate([gs[0], gs[1], gs[0]], axis=0))
+
+
+def widen(walls, wide, tall):
+    for k in range(walls.shape[0]):
+        high, low = split(walls[k])
+        wide[k] = jnp.concatenate([high, high, low], axis=1)
+        tall[k] = jnp.concatenate([high, low, high], axis=0)
 
 
 class Sweep:
@@ -163,7 +171,7 @@
 def line_kernel(
     rates, faces, neighbours, side_in, old, library_in, walls_in, blocks_in,
     out, sides_out, index_out, missed_out,
-    side, library, walls, blocks, index, halo, sides, values, ph, plo, gh, glo,
+    side, library, walls, wide, tall, blocks, index, halo, sides, values, ph, plo, gh, glo,
     local_sem, index_send, index_recv, halo_send, halo_recv, side_send, side_recv,
 ):
     n = lax.axis_size("wall")
@@ -233,9 +241,10 @@
         copy.start()
     for load in loads[:2]:
         load.wait()
+    widen(walls, wide, tall)
     for copy in index_copies:
         copy.wait()
-    line = Line(index, mine, library, walls)
+    line = Line(index, mine, library, walls, wide, tall)
     stores = (ph, plo, gh, glo)
     low, high = line.block(0), line.block(top)
     missed = jnp.zeros((1, 1), F32)
@@ -244,8 +253,8 @@
         j = top - i
         (x, y), off = invert([low, high])
         missed = missed + off
-        low = line.block(i + 1) - keep(i, x, line.face(i + 1), stores)
-        high = line.block(j - 1) - keep(j, y, line.face(j), stores)
+        low = line.block(i + 1) - keep(i, x, line.coupling(i + 1), stores)
+        high = line.block(j - 1) - keep(j, y, line.coupling(j), stores)
         if i == max(0, half - 3):
             for load in loads[2:]:
                 load.wait()
@@ -262,24 +271,30 @@
             side_copies = spread(sides, side_send, side_recv)
     for copy in side_copies:
         copy.wait()
+    handed = [
+        pltpu.make_async_copy(sides, sides_out, local_sem.at[4]),
+        pltpu.make_async_copy(index, index_out, local_sem.at[5]),
+    ]
+    for copy in handed:
+        copy.start()
     sweep = Sweep(count, stores, lambda i: sides[i // mine, i % mine])
     sweep.forward()
     (y,), off = invert([high])
     missed = missed + off
-    low = low - keep(half, y, line.face(half), stores)
+    low = low - keep(half, y, line.coupling(half), stores)
     (x,), off = invert([low], 1)
     missed = missed + off
     sweep.back(x, values)
     for e in range(mine):
         out[0, 0, e] = values[place * mine + e]
-    sides_out[...] = sides[...]
-    index_out[...] = index[...]
+    for copy in handed:
+        copy.wait()
     missed_out[...] = jnp.broadcast_to(missed, missed_out.shape)
 
 
 def check_kernel(
     missed, fast, sides_in, index_in, library_in, walls_in,
-    out, sides, index, library, walls, values, block, inverse, ph, plo, gh, glo,
+    out, sides, index, library, walls, wide, tall, values, block, inverse, ph, plo, gh, glo,
 ):
     out[...] = fast[...]
 
@@ -293,7 +308,8 @@
         count = n * mine
         half = count // 2
         place = lax.axis_index("wall")
-        line = Line(index, mine, library, walls)
+        widen(walls, wide, tall)
+        line = Line(index, mine, library, walls, wide, tall)
         stores = (ph, plo, gh, glo)
 
         def exact(a):
@@ -305,11 +321,11 @@
         high = line.block(count - 1)
         for i in range(half - 1):
             j = count - 1 - i
-            low = line.block(i + 1) - keep(i, exact(low), line.face(i + 1), stores)
-            high = line.block(j - 1) - keep(j, exact(high), line.face(j), stores)
+            low = line.block(i + 1) - keep(i, exact(low), line.coupling(i + 1), stores)
+            high = line.block(j - 1) - keep(j, exact(high), line.coupling(j), stores)
         sweep = Sweep(count, stores, lambda i: sides[i // mine, i % mine])
         sweep.forward()
-        low = low - keep(half, exact(high), line.face(half), stores)
+        low = low - keep(half, exact(high), line.coupling(half), stores)
         sweep.back(exact(low), values)
         for e in range(mine):
             out[0, 0, e] = values[place * mine + e]
@@ -341,18 +357,20 @@
         line_kernel,
         out_shape=[one, all_sides, all_rows, jax.ShapeDtypeStruct((8, 128), F32)],
         in_specs=[smem] * 3 + [free] * 5,
-        out_specs=[vmem] * 4,
+        out_specs=[vmem, free, free, vmem],
         scratch_shapes=[
             pltpu.VMEM((mine,) + tail, F32),
             pltpu.VMEM(element_library.shape, F32),
             pltpu.VMEM(wall_library.shape, F32),
+            pltpu.VMEM((wall_library.shape[0], size, 3 * size), BF16),
+            pltpu.VMEM((wall_library.shape[0], 3 * size, size), BF16),
             pltpu.VMEM(face_library.shape, F32),
             pltpu.VMEM(all_rows.shape, jnp.int32),
             pltpu.VMEM((4, mine) + tail, F32),
             pltpu.VMEM(all_sides.shape, F32),
             pltpu.VMEM((count,) + tail, F32),
             *stores,
-            pltpu.SemaphoreType.DMA((4,)),
+            pltpu.SemaphoreType.DMA((6,)),
             pltpu.SemaphoreType.DMA((n - 1,)),
             pltpu.SemaphoreType.DMA((n - 1,)),
             pltpu.SemaphoreType.DMA((4,)),
@@ -378,6 +396,8 @@
             pltpu.VMEM(all_rows.shape, jnp.int32),
             pltpu.VMEM(element_library.shape, F32),
             pltpu.VMEM(wall_library.shape, F32),
+            pltpu.VMEM((wall_library.shape[0], size, 3 * size), BF16),
+            pltpu.VMEM((wall_library.shape[0], 3 * size, size), BF16),
             pltpu.VMEM((count,) + tail, F32),
             pltpu.VMEM((size, size), F32),
             pltpu.VMEM((size, size), F32),

time: 462 us -> 460 us (level)
  the two profiles are of different devices: /device:TPU:0 before, /device:TPU:19 now
where the time goes in v5:
time: 460 us; the launch traced here: 458 us
  Pallas kernels  458 us (100%)
    pallas_call x1, Pallas kernels, on_device(): pl.pallas_call(check_kernel, out_shape=one, in_specs=[vmem] * 2 + [free]...  421 us
    pallas_call x1, Pallas kernels, on_device(): pl.pallas_call(line_kernel, out_shape=[one, all_sides, all_rows, jax.Shap...  37.3 us

profile of v5, /device:TPU:19, one launch (start us, length us, event | category | flops | bytes accessed | tf_op | source)
XLA Modules:
  0.0 458.0 jit_solution(740649888089624915)
XLA Ops:
  0.0 37.3 %line.1 = (f32[1,1,2,64,320]{4,3,2,1,0:T(8,128)}, f32[4,2,64,320]{3,2,1,0:T(8,128)}, s32[4,8,128]{2,1,0:T(8,128)}, f32[8,128]{1,0:T(8,128)}) custom-call(s32[1,1,2]{2,1,0:T(1,128)} %rates.1, s32[1,1,2,2]{3,2,1,0:T(2,128)} %faces.1, s32[1,1,2,4]{3,2,1,0:T(2,128)} %neighbours.1, f32[1,1,2,64,320]{4,3,2,1,0:T(8,128)} %side_in.1, f32[1,1,2,64,320]{4,3,2,1,0:T(8,128)} %old.1, ...), custom_call_target="tpu_custom_call" | custom-call | tf_op jit(solution)/shard_map/line/pallas_call | solution.py:356
  37.3 420.7 %check.1 = f32[1,1,2,64,320]{4,3,2,1,0:T(8,128)} custom-call(f32[8,128]{1,0:T(8,128)} %get-tuple-element.9.missed, f32[1,1,2,64,320]{4,3,2,1,0:T(8,128)} %get-tuple-element.10.fast, f32[4,2,64,320]{3,2,1,0:T(8,128)} %get-tuple-element.11.sides_in, s32[4,8,128]{2,1,0:T(8,128)} %get-tuple-element.12.index_in, f32[8,320]{1,0:T(8,128)} %library_in.3, ...), custom_call_target="tpu_custom_call" | custom-call | tf_op jit(solution)/shard_map/check/pallas_call | solution.py:389

commit v6 on v5

--- a/solution.py
+++ b/solution.py
@@ -294,9 +294,16 @@
 
 def check_kernel(
     missed, fast, sides_in, index_in, library_in, walls_in,
-    out, sides, index, library, walls, wide, tall, values, block, inverse, ph, plo, gh, glo,
+    out, sides, index, library, walls, wide, tall, values, block, inverse, ph, plo, gh, glo, sem,
 ):
-    out[...] = fast[...]
+    passed = [
+        pltpu.make_async_copy(fast.at[0, 0, e], out.at[0, 0, e], sem.at[e])
+        for e in range(sides.shape[1])
+    ]
+    for copy in passed:
+        copy.start()
+    for copy in passed:
+        copy.wait()
 
     @pl.when(jnp.logical_not(missed[0:1, 0:1][0, 0] < 0.5))
     def _():
@@ -328,7 +335,7 @@
         low = low - keep(half, exact(high), line.coupling(half), stores)
         sweep.back(exact(low), values)
         for e in range(mine):
-            out[0, 0, e] = values[place * mine + e]
+            pltpu.sync_copy(values.at[place * mine + e], out.at[0, 0, e])
 
 
 def on_device(
@@ -389,8 +396,8 @@
     return pl.pallas_call(
         check_kernel,
         out_shape=one,
-        in_specs=[vmem] * 2 + [free] * 4,
-        out_specs=vmem,
+        in_specs=[vmem] + [free] * 5,
+        out_specs=free,
         scratch_shapes=[
             pltpu.VMEM(all_sides.shape, F32),
             pltpu.VMEM(all_rows.shape, jnp.int32),
@@ -402,6 +409,7 @@
             pltpu.VMEM((size, size), F32),
             pltpu.VMEM((size, size), F32),
             *stores,
+            pltpu.SemaphoreType.DMA((mine,)),
         ],
         compiler_params=pltpu.CompilerParams(vmem_limit_bytes=60 * 1024 * 1024),
         name="check",

time: 460 us -> 467 us (1.015)
  the two profiles are of different devices: /device:TPU:19 before, /device:TPU:11 now
where the time goes in v6:
time: 467 us; the launch traced here: 465 us
  Pallas kernels  465 us (100%)
    pallas_call x1, Pallas kernels, on_device(): pl.pallas_call(check_kernel, out_shape=one, in_specs=[vmem] + [free] * 5,...  427 us
    pallas_call x1, Pallas kernels, on_device(): pl.pallas_call(line_kernel, out_shape=[one, all_sides, all_rows, jax.Shap...  37.3 us

profile of v6, /device:TPU:11, one launch (start us, length us, event | category | flops | bytes accessed | tf_op | source)
XLA Modules:
  0.0 464.8 jit_solution(8825308102711581702)
XLA Ops:
  0.0 37.3 %line.1 = (f32[1,1,2,64,320]{4,3,2,1,0:T(8,128)}, f32[4,2,64,320]{3,2,1,0:T(8,128)}, s32[4,8,128]{2,1,0:T(8,128)}, f32[8,128]{1,0:T(8,128)}) custom-call(s32[1,1,2]{2,1,0:T(1,128)} %rates.1, s32[1,1,2,2]{3,2,1,0:T(2,128)} %faces.1, s32[1,1,2,4]{3,2,1,0:T(2,128)} %neighbours.1, f32[1,1,2,64,320]{4,3,2,1,0:T(8,128)} %side_in.1, f32[1,1,2,64,320]{4,3,2,1,0:T(8,128)} %old.1, ...), custom_call_target="tpu_custom_call" | custom-call | tf_op jit(solution)/shard_map/line/pallas_call | solution.py:363
  37.3 427.3 %check.1 = f32[1,1,2,64,320]{4,3,2,1,0:T(8,128)} custom-call(f32[8,128]{1,0:T(8,128)} %get-tuple-element.9.missed, f32[1,1,2,64,320]{4,3,2,1,0:T(8,128)} %get-tuple-element.10.fast, f32[4,2,64,320]{3,2,1,0:T(8,128)} %get-tuple-element.11.sides_in, s32[4,8,128]{2,1,0:T(8,128)} %get-tuple-element.12.index_in, f32[8,320]{1,0:T(8,128)} %library_in.3, ...), custom_call_target="tpu_custom_call" | custom-call | tf_op jit(solution)/shard_map/check/pallas_call | solution.py:396
